TPU v7x, 128 devices: a whole 4x4x4 slice. The times are simulated.
128 devices in a mesh: grp: 16 (over z, y), tp: 8 (over x, core).
Axes of the slice: x: 4, y: 4, z: 4, core: 2. Of those that a mesh axis runs over, the one named last changes fastest.
Arguments:
- queries: bfloat16 [4096, 8192], P('grp', 'tp'), may hold values from -64 to 64
- row_counts: int32 [16], P('grp'), may hold values from 128 to 256, as said below
- owners: int32 [4096], P('grp'), may hold values from 0 to 15, as said below
- lengths: int32 [4096], P('grp'), may hold values from 1601 to 6404, as said below
- img_keys: bfloat16 [16, 6404, 1024], P('grp', None, 'tp'), may hold values from -12 to 12
- img_values: bfloat16 [16, 6404, 1024], P('grp', None, 'tp'), may hold values from -30 to 30
- out_weight: bfloat16 [8192, 8192], P(None, 'tp'), may hold values from -0.0625 to 0.0625
- gate_scalar: float32 [1], replicated, may hold values from 0.3 to 1.5
Outputs:
- mixed: bfloat16 [4096, 8192], P('grp', 'tp')
Inputs may be any that keep to these rules, and one draw needn't show every extreme that they name: `row_counts`: rows of a group with local index below its count are live, the others give zero output; some group is full. `owners`: among the 256 rows of one group at most 32 name the same owner; some owner is named by exactly 32 live rows of every group. `lengths`: a multiple of 1601.
All inputs are finite; a program needn't handle non-finite values.
Results may differ from a plain program's by a relative error of at most 0.0053.
Values may be sent and summed in bfloat16 or wider, within the bound.
No kernel may reach another device: no remote copies, remote signals or barrier semaphores. Data moves between devices by JAX's collectives and lax.ppermute only.
A program may use at most 128 MiB of HBM per device.

v0:
```python
import jax
import jax.numpy as jnp
from jax import lax
from jax.sharding import PartitionSpec as P

HD = 128
CAP = 32


def shards(queries, row_counts, owners, lengths, img_keys, img_values, out_weight, gate_scalar):
    row_total = queries.shape[0]
    feature_width = queries.shape[1]
    groups = lax.axis_size("grp")
    kv_local = img_keys.shape[2] // HD
    share = feature_width // HD // kv_local
    cache_len = img_keys.shape[1]
    key_cache = img_keys[0].reshape(cache_len, kv_local, HD)
    value_cache = img_values[0].reshape(cache_len, kv_local, HD)
    gate_factor = jnp.tanh(gate_scalar[0])
    live_rows = jnp.arange(row_total, dtype=jnp.int32) < row_counts[0]
    owner_hits = (
        (owners[:, None] == jnp.arange(groups, dtype=jnp.int32)[None, :]) & live_rows[:, None]
    ).astype(jnp.int32)
    earlier = jnp.cumsum(owner_hits, axis=0) - owner_hits
    position = jnp.sum(earlier * owner_hits, axis=1)
    target = jnp.where(live_rows, owners * CAP + position, groups * CAP)
    send_queries = (
        jnp.zeros((groups * CAP, feature_width), jnp.bfloat16).at[target].set(queries, mode="drop")
    )
    send_lengths = jnp.zeros((groups * CAP,), jnp.int32).at[target].set(lengths, mode="drop")
    send_queries = send_queries.reshape(groups, CAP, feature_width)
    send_lengths = send_lengths.reshape(groups, CAP)

    def attend_block(block_pair):
        query_block, length_block = block_pair
        count = query_block.shape[0]
        grouped = query_block.reshape(count, kv_local, share, HD)
        scores = jnp.einsum(
            "bkgd,lkd->bkgl", grouped, key_cache, preferred_element_type=jnp.float32
        ) * HD ** (-0.5)
        visible = (
            jnp.arange(cache_len, dtype=jnp.int32)[None, None, None, :]
            < jnp.maximum(length_block, 1)[:, None, None, None]
        )
        scores = jnp.where(visible, scores, -jnp.inf)
        row_peak = jnp.max(scores, axis=-1, keepdims=True)
        weights = jnp.exp(scores - row_peak)
        total_weight = jnp.sum(weights, axis=-1)
        combined = jnp.einsum(
            "bkgl,lkd->bkgd",
            weights.astype(jnp.bfloat16),
            value_cache,
            preferred_element_type=jnp.float32,
        )
        combined = combined / total_weight[..., None]
        return combined.astype(jnp.bfloat16).reshape(count, feature_width)

    received_queries = lax.all_to_all(send_queries, "grp", split_axis=0, concat_axis=0, tiled=True)
    received_lengths = lax.all_to_all(send_lengths, "grp", split_axis=0, concat_axis=0, tiled=True)
    per_source = received_queries.shape[1]
    slot_count = groups * per_source
    step_rows = 2 * per_source
    block_count = slot_count // step_rows
    blocked = (
        received_queries.reshape(block_count, step_rows, feature_width),
        received_lengths.reshape(block_count, step_rows),
    )
    attention = lax.map(attend_block, blocked).reshape(slot_count, feature_width)
    returned = lax.all_to_all(
        attention.reshape(groups, per_source, feature_width),
        "grp",
        split_axis=0,
        concat_axis=0,
        tiled=True,
    )
    flat_returned = returned.reshape(groups * CAP, returned.shape[2])
    picked = flat_returned[jnp.minimum(target, groups * CAP - 1)]
    picked = jnp.where(live_rows[:, None], picked, jnp.zeros_like(picked))
    projected = jnp.dot(
        lax.all_gather(picked, "tp", axis=1, tiled=True),
        out_weight,
        preferred_element_type=jnp.float32,
    )
    mixed = (gate_factor * projected).astype(jnp.bfloat16)
    return mixed


def solution(mesh):
    placed = (
        P("grp", "tp"),
        P("grp"),
        P("grp"),
        P("grp"),
        P("grp", None, "tp"),
        P("grp", None, "tp"),
        P(None, "tp"),
        P(),
    )
    return jax.shard_map(
        shards, mesh=mesh, in_specs=placed, out_specs=P("grp", "tp"), check_vma=False
    )
```

profile of v0, /device:TPU:1, one launch (start us, length us, event | category | flops | bytes accessed | tf_op | source)
XLA Modules:
  0.0 208.7 jit_solution(7715768290295809932)
XLA Ops:
  12.4 8.6 %all-to-all-start = ((s32[16,1,32]{2,1,0:T(1,128)}), s32[16,1,32]{2,1,0:T(1,128)S(1)}, u32[]{:S(2)}, u32[]{:S(2)}) async-start(s32[16,1,32]{2,1,0:T(1,128)} %all_to_all.12), calls=%async_computation | async-start | bytes 16384 | tf_op jit(solution)/shard_map/all_to_all | solution.py:59
  21.0 3.2 %scatter_custom_fusion.1 = bf16[512,1024]{1,0:T(8,128)(2,1)} fusion(s32[256]{0:T(256)S(1)} %get-tuple-element.53, bf16[256,1024]{1,0:T(8,128)(2,1)} %param.10, bf16[]{:T(256)} %constant.19.clone.1), kind=kCustom, calls=%fused_computation.24 | custom fusion | bytes 1049088 | tf_op jit(solution)/shard_map/scatter | solution.py:28
  24.2 3.2 %all-to-all-done = s32[16,1,32]{2,1,0:T(1,128)S(1)} async-done(((s32[16,1,32]{2,1,0:T(1,128)}), s32[16,1,32]{2,1,0:T(1,128)S(1)}, u32[]{:S(2)}, u32[]{:S(2)}) %all-to-all-start) | async-done | bytes 2080 | tf_op jit(solution)/shard_map/all_to_all | solution.py:59
  27.3 4.3 %all-to-all-start.1 = ((bf16[16,32,1024]{2,1,0:T(8,128)(2,1)}), bf16[16,32,1024]{2,1,0:T(8,128)(2,1)}, u32[]{:S(2)}, u32[]{:S(2)}) async-start(bf16[16,32,1024]{2,1,0:T(8,128)(2,1)} %bitcast.16), calls=%async_computation.1 | async-start | bytes 2097152 | tf_op jit(solution)/shard_map/all_to_all | solution.py:58
  32.9 13.7 %all-to-all-done.1 = bf16[16,32,1024]{2,1,0:T(8,128)(2,1)} async-done(((bf16[16,32,1024]{2,1,0:T(8,128)(2,1)}), bf16[16,32,1024]{2,1,0:T(8,128)(2,1)}, u32[]{:S(2)}, u32[]{:S(2)}) %all-to-all-start.1) | async-done | bytes 1048608 | tf_op jit(solution)/shard_map/all_to_all | solution.py:58
  46.6 88.2 %while.10 = (s32[]{:T(128)}, bf16[8,64,1024]{2,1,0:T(8,128)(2,1)}, s32[8,64]{1,0:T(8,128)S(1)}, bf16[8,64,1024]{2,1,0:T(8,128)(2,1)}, bf16[6404,1,128]{2,0,1:T(8...) while((s32[]{:T(128)}, bf16[8,64,1024]{2,1,0:T(8,128)(2,1)}, s32[8,64]{1,0:T(8,128)S(1)}, ...), condition=%wide.region_8.9_spmd, body=%wide.region_5.8_spmd.sunk | while | flops 1702262016 | bytes 51324784 | solution.py:68
  47.9 5.1 %fusion.56 = (f32[64,8]{1,0:T(8,128)S(1)}, f32[64,1,8,6404]{3,2,0,1:T(8,128)S(1)}) fusion(bf16[64,8,128]{2,1,0:T(8,128)(2,1)S(1)} %bitcast.112, bf16[6404,1,128]{2,0,1:T(8,128)(2,1)} %get-tuple-element.113, pred[64,6404]{1,0:T(8,128)(4,1)S(1)} %iota_compare_fusion.5), kind=kOutput, calls=%fused_computation.46.clone.1 | convolution fusion | flops 849221120 | bytes 15297792 | tf_op jit(solution)/shard_map/while/body/eval_jaxpr/bkgd,lkd->bkgl/dot_general | solution.py:38
  53.0 1.9 fusion.57
  54.9 2.0 fusion.58
  58.9 5.1 %fusion.56 = (f32[64,8]{1,0:T(8,128)S(1)}, f32[64,1,8,6404]{3,2,0,1:T(8,128)S(1)}) fusion(bf16[64,8,128]{2,1,0:T(8,128)(2,1)S(1)} %bitcast.112, bf16[6404,1,128]{2,0,1:T(8,128)(2,1)} %get-tuple-element.113, pred[64,6404]{1,0:T(8,128)(4,1)S(1)} %iota_compare_fusion.5), kind=kOutput, calls=%fused_computation.46.clone.1 | convolution fusion | flops 849221120 | bytes 15297792 | tf_op jit(solution)/shard_map/while/body/eval_jaxpr/bkgd,lkd->bkgl/dot_general | solution.py:38
  64.1 1.9 fusion.57
  66.0 2.0 fusion.58
  70.0 5.1 %fusion.56 = (f32[64,8]{1,0:T(8,128)S(1)}, f32[64,1,8,6404]{3,2,0,1:T(8,128)S(1)}) fusion(bf16[64,8,128]{2,1,0:T(8,128)(2,1)S(1)} %bitcast.112, bf16[6404,1,128]{2,0,1:T(8,128)(2,1)} %get-tuple-element.113, pred[64,6404]{1,0:T(8,128)(4,1)S(1)} %iota_compare_fusion.5), kind=kOutput, calls=%fused_computation.46.clone.1 | convolution fusion | flops 849221120 | bytes 15297792 | tf_op jit(solution)/shard_map/while/body/eval_jaxpr/bkgd,lkd->bkgl/dot_general | solution.py:38
  75.1 1.9 fusion.57
  77.0 2.0 fusion.58
  81.0 5.1 %fusion.56 = (f32[64,8]{1,0:T(8,128)S(1)}, f32[64,1,8,6404]{3,2,0,1:T(8,128)S(1)}) fusion(bf16[64,8,128]{2,1,0:T(8,128)(2,1)S(1)} %bitcast.112, bf16[6404,1,128]{2,0,1:T(8,128)(2,1)} %get-tuple-element.113, pred[64,6404]{1,0:T(8,128)(4,1)S(1)} %iota_compare_fusion.5), kind=kOutput, calls=%fused_computation.46.clone.1 | convolution fusion | flops 849221120 | bytes 15297792 | tf_op jit(solution)/shard_map/while/body/eval_jaxpr/bkgd,lkd->bkgl/dot_general | solution.py:38
  88.0 2.0 fusion.58
  92.1 5.1 %fusion.56 = (f32[64,8]{1,0:T(8,128)S(1)}, f32[64,1,8,6404]{3,2,0,1:T(8,128)S(1)}) fusion(bf16[64,8,128]{2,1,0:T(8,128)(2,1)S(1)} %bitcast.112, bf16[6404,1,128]{2,0,1:T(8,128)(2,1)} %get-tuple-element.113, pred[64,6404]{1,0:T(8,128)(4,1)S(1)} %iota_compare_fusion.5), kind=kOutput, calls=%fused_computation.46.clone.1 | convolution fusion | flops 849221120 | bytes 15297792 | tf_op jit(solution)/shard_map/while/body/eval_jaxpr/bkgd,lkd->bkgl/dot_general | solution.py:38
  97.2 1.9 fusion.57
  99.1 2.0 fusion.58
  103.1 5.1 %fusion.56 = (f32[64,8]{1,0:T(8,128)S(1)}, f32[64,1,8,6404]{3,2,0,1:T(8,128)S(1)}) fusion(bf16[64,8,128]{2,1,0:T(8,128)(2,1)S(1)} %bitcast.112, bf16[6404,1,128]{2,0,1:T(8,128)(2,1)} %get-tuple-element.113, pred[64,6404]{1,0:T(8,128)(4,1)S(1)} %iota_compare_fusion.5), kind=kOutput, calls=%fused_computation.46.clone.1 | convolution fusion | flops 849221120 | bytes 15297792 | tf_op jit(solution)/shard_map/while/body/eval_jaxpr/bkgd,lkd->bkgl/dot_general | solution.py:38
  108.2 1.9 fusion.57
  110.1 2.0 fusion.58
  114.1 5.1 %fusion.56 = (f32[64,8]{1,0:T(8,128)S(1)}, f32[64,1,8,6404]{3,2,0,1:T(8,128)S(1)}) fusion(bf16[64,8,128]{2,1,0:T(8,128)(2,1)S(1)} %bitcast.112, bf16[6404,1,128]{2,0,1:T(8,128)(2,1)} %get-tuple-element.113, pred[64,6404]{1,0:T(8,128)(4,1)S(1)} %iota_compare_fusion.5), kind=kOutput, calls=%fused_computation.46.clone.1 | convolution fusion | flops 849221120 | bytes 15297792 | tf_op jit(solution)/shard_map/while/body/eval_jaxpr/bkgd,lkd->bkgl/dot_general | solution.py:38
  121.1 2.0 fusion.58
  125.1 5.1 %fusion.56 = (f32[64,8]{1,0:T(8,128)S(1)}, f32[64,1,8,6404]{3,2,0,1:T(8,128)S(1)}) fusion(bf16[64,8,128]{2,1,0:T(8,128)(2,1)S(1)} %bitcast.112, bf16[6404,1,128]{2,0,1:T(8,128)(2,1)} %get-tuple-element.113, pred[64,6404]{1,0:T(8,128)(4,1)S(1)} %iota_compare_fusion.5), kind=kOutput, calls=%fused_computation.46.clone.1 | convolution fusion | flops 849221120 | bytes 15297792 | tf_op jit(solution)/shard_map/while/body/eval_jaxpr/bkgd,lkd->bkgl/dot_general | solution.py:38
  130.2 1.9 fusion.57
  132.1 2.0 fusion.58
  134.9 4.6 %all-to-all-start.2 = ((bf16[16,32,1024]{2,1,0:T(8,128)(2,1)}), bf16[16,32,1024]{2,1,0:T(8,128)(2,1)S(1)}, u32[]{:S(2)}, u32[]{:S(2)}) async-start(bf16[16,32,1024]{2,1,0:T(8,128)(2,1)} %bitcast.113), calls=%async_computation.2 | async-start | bytes 2097152 | tf_op jit(solution)/shard_map/all_to_all | solution.py:69
  139.8 14.7 %all-to-all-done.2 = bf16[16,32,1024]{2,1,0:T(8,128)(2,1)S(1)} async-done(((bf16[16,32,1024]{2,1,0:T(8,128)(2,1)}), bf16[16,32,1024]{2,1,0:T(8,128)(2,1)S(1)}, u32[]{:S(2)}, u32[]{:S(2)}) %all-to-all-start.2) | async-done | bytes 1048608 | tf_op jit(solution)/shard_map/all_to_all | solution.py:69
  157.3 32.2 %all-gather.2.cloned.1.call-done = bf16[256,8192]{1,0:T(8,128)(2,1)} async-done(((bf16[256,1024]{1,0:T(8,128)(2,1)}), bf16[256,8192]{1,0:T(8,128)(2,1)}) %all-gather.2.cloned.1.call-update) | async-done | bytes 4194320 | tf_op jit(solution)/shard_map/all_gather | solution.py:80
  189.5 12.3 %fusion.30 = bf16[256,1024]{1,0:T(8,128)(2,1)} fusion(bf16[256,8192]{1,0:T(8,128)(2,1)} %all-gather.2.cloned.1.call-done, bf16[8192,1024]{1,0:T(8,128)(2,1)} %param.16, f32[]{:T(128)} %bitcast.12), kind=kOutput, calls=%fused_computation.23 | convolution fusion | flops 4295491584 | bytes 21495812 | tf_op jit(solution)/shard_map/dot_general | solution.py:79
  (86 shorter events, 28.3 us)
Async XLA Ops:
  12.4 14.9 %all-to-all-start = ((s32[16,1,32]{2,1,0:T(1,128)}), s32[16,1,32]{2,1,0:T(1,128)S(1)}, u32[]{:S(2)}, u32[]{:S(2)}) async-start(s32[16,1,32]{2,1,0:T(1,128)} %all_to_all.12), calls=%async_computation | async-start | bytes 16384 | tf_op jit(solution)/shard_map/all_to_all | solution.py:59
  27.3 19.3 %all-to-all-start.1 = ((bf16[16,32,1024]{2,1,0:T(8,128)(2,1)}), bf16[16,32,1024]{2,1,0:T(8,128)(2,1)}, u32[]{:S(2)}, u32[]{:S(2)}) async-start(bf16[16,32,1024]{2,1,0:T(8,128)(2,1)} %bitcast.16), calls=%async_computation.1 | async-start | bytes 2097152 | tf_op jit(solution)/shard_map/all_to_all | solution.py:58
  47.9 7.0 %copy-start = (bf16[6404,1,128]{2,0,1:T(8,128)(2,1)S(1)}, bf16[6404,1,128]{2,0,1:T(8,128)(2,1)}, u32[]{:S(2)}) copy-start(bf16[6404,1,128]{2,0,1:T(8,128)(2,1)} %get-tuple-element.114) | copy-start | bytes 4918276 | tf_op jit(solution)/shard_map/while
  58.9 7.0 %copy-start = (bf16[6404,1,128]{2,0,1:T(8,128)(2,1)S(1)}, bf16[6404,1,128]{2,0,1:T(8,128)(2,1)}, u32[]{:S(2)}) copy-start(bf16[6404,1,128]{2,0,1:T(8,128)(2,1)} %get-tuple-element.114) | copy-start | bytes 4918276 | tf_op jit(solution)/shard_map/while
  70.0 7.0 %copy-start = (bf16[6404,1,128]{2,0,1:T(8,128)(2,1)S(1)}, bf16[6404,1,128]{2,0,1:T(8,128)(2,1)}, u32[]{:S(2)}) copy-start(bf16[6404,1,128]{2,0,1:T(8,128)(2,1)} %get-tuple-element.114) | copy-start | bytes 4918276 | tf_op jit(solution)/shard_map/while
  81.0 7.0 %copy-start = (bf16[6404,1,128]{2,0,1:T(8,128)(2,1)S(1)}, bf16[6404,1,128]{2,0,1:T(8,128)(2,1)}, u32[]{:S(2)}) copy-start(bf16[6404,1,128]{2,0,1:T(8,128)(2,1)} %get-tuple-element.114) | copy-start | bytes 4918276 | tf_op jit(solution)/shard_map/while
  92.0 7.0 %copy-start = (bf16[6404,1,128]{2,0,1:T(8,128)(2,1)S(1)}, bf16[6404,1,128]{2,0,1:T(8,128)(2,1)}, u32[]{:S(2)}) copy-start(bf16[6404,1,128]{2,0,1:T(8,128)(2,1)} %get-tuple-element.114) | copy-start | bytes 4918276 | tf_op jit(solution)/shard_map/while
  103.1 7.0 %copy-start = (bf16[6404,1,128]{2,0,1:T(8,128)(2,1)S(1)}, bf16[6404,1,128]{2,0,1:T(8,128)(2,1)}, u32[]{:S(2)}) copy-start(bf16[6404,1,128]{2,0,1:T(8,128)(2,1)} %get-tuple-element.114) | copy-start | bytes 4918276 | tf_op jit(solution)/shard_map/while
  114.1 7.0 %copy-start = (bf16[6404,1,128]{2,0,1:T(8,128)(2,1)S(1)}, bf16[6404,1,128]{2,0,1:T(8,128)(2,1)}, u32[]{:S(2)}) copy-start(bf16[6404,1,128]{2,0,1:T(8,128)(2,1)} %get-tuple-element.114) | copy-start | bytes 4918276 | tf_op jit(solution)/shard_map/while
  125.1 7.0 %copy-start = (bf16[6404,1,128]{2,0,1:T(8,128)(2,1)S(1)}, bf16[6404,1,128]{2,0,1:T(8,128)(2,1)}, u32[]{:S(2)}) copy-start(bf16[6404,1,128]{2,0,1:T(8,128)(2,1)} %get-tuple-element.114) | copy-start | bytes 4918276 | tf_op jit(solution)/shard_map/while
  134.9 19.6 %all-to-all-start.2 = ((bf16[16,32,1024]{2,1,0:T(8,128)(2,1)}), bf16[16,32,1024]{2,1,0:T(8,128)(2,1)S(1)}, u32[]{:S(2)}, u32[]{:S(2)}) async-start(bf16[16,32,1024]{2,1,0:T(8,128)(2,1)} %bitcast.113), calls=%async_computation.2 | async-start | bytes 2097152 | tf_op jit(solution)/shard_map/all_to_all | solution.py:69
  139.5 50.0 %all-gather.2.cloned.1.call-start = ((), (), s32[]{:S(2)}) async-start(), calls=%async_computation.3 | async-start | bytes 4718592 | tf_op jit(solution)/shard_map/all_gather | solution.py:80
Sparse Core Ops, SparseCore 0:
  156.8 32.7 all-gather.1
where the time goes:
time: 210 us; the launch traced here: 209 us
  matrix products  69.3 us (33%)
  waiting for transfers between devices  63.9 us (30%)
  other arithmetic  21.9 us (10%)
  local copies, waits for them, and re-layouts  20.7 us (10%)
  starting transfers between devices  17.8 us (8%)
  between operations  14.8 us (7%)
    dot_general x8, matrix products, attend_block(): jnp.einsum('bkgd,lkd->bkgl', grouped, key_cache, preferred_element_type=j...  40.8 us
    all_gather x1, waiting for transfers between devices, shards(): lax.all_gather(picked, 'tp', axis=1, tiled=True)  32.2 us
    dot_general x8, matrix products, attend_block(): jnp.einsum('bkgl,lkd->bkgd', weights.astype(jnp.bfloat16), value_cache, p...  16.1 us
    reduce_sum x8, other arithmetic, attend_block(): total_weight = jnp.sum(weights, axis=-1)  15.2 us
    all_to_all x1, waiting for transfers between devices, shards(): lax.all_to_all(attention.reshape(groups, per_source, feature_width), 'grp...  14.7 us
    all_to_all x1, waiting for transfers between devices, shards(): lax.all_to_all(send_queries, 'grp', split_axis=0, concat_axis=0, tiled=True)  13.7 us
    dot_general x1, matrix products, shards(): jnp.dot(lax.all_gather(picked, 'tp', axis=1, tiled=True), out_weight, pre...  12.3 us
    all_to_all x1, starting transfers between devices, shards(): lax.all_to_all(send_lengths, 'grp', split_axis=0, concat_axis=0, tiled=True)  8.6 us
  transfers between devices with their start and end apart: 4, of which 4 were waited for; matrix products, arithmetic and copies ran while one was open for 2% of the time, Pallas kernels for 0%

commit v1 on v0

v1 whole, which is shorter than its diff:
```python
import functools

import jax
import jax.numpy as jnp
from jax import lax
from jax.experimental import pallas as pl
from jax.experimental.pallas import tpu as pltpu
from jax.sharding import PartitionSpec as P

f32, bf16, i32 = jnp.float32, jnp.bfloat16, jnp.int32
HD = 128
CAP = 32
TILE = 1601
TILES = 4
TP = 1664
HUGE = 1e30
VM = pl.BlockSpec(memory_space=pltpu.VMEM)
SM = pl.BlockSpec(memory_space=pltpu.SMEM)


def dispatch_body(owners, lengths, counts, queries, send, back):
    rows = queries.shape[0]
    width = queries.shape[1]
    slots = send.shape[0]
    i = lax.broadcasted_iota(i32, (rows, rows), 0)
    j = lax.broadcasted_iota(i32, (rows, rows), 1)
    own_j = jnp.broadcast_to(owners[...].astype(f32), (rows, rows))
    own_i = own_j.T
    same = (own_i == own_j) & (i < j) & (i < counts[0])
    pos = jnp.sum(jnp.where(same, 1.0, 0.0), axis=0, keepdims=True)
    live = lax.broadcasted_iota(i32, (1, rows), 1) < counts[0]
    target = jnp.where(live, owners[...].astype(f32) * CAP + pos, -1.0)
    slot = lax.broadcasted_iota(i32, (slots, rows), 0).astype(f32)
    pick = jnp.where(jnp.broadcast_to(target, (slots, rows)) == slot, 1.0, 0.0).astype(bf16)
    send[:, :width] = jnp.dot(pick, queries[...], preferred_element_type=f32).astype(bf16)
    seen = sum(jnp.where(lengths[...] > k * TILE, 1.0, 0.0) for k in range(TILES))
    seen = jnp.broadcast_to(seen, (HD, rows)).T.astype(bf16)
    send[:, width:] = jnp.dot(pick, seen, preferred_element_type=f32).astype(bf16)
    target_i = jnp.broadcast_to(target, (HD, rows)).T
    lane = lax.broadcasted_iota(i32, (rows, HD), 1).astype(f32)
    for k in range(slots // HD):
        back[:, k * HD : (k + 1) * HD] = jnp.where(target_i == lane + k * HD, 1.0, 0.0).astype(bf16)


def dispatch(owners, lengths, counts, queries, slots):
    rows, width = queries.shape
    return pl.pallas_call(
        dispatch_body,
        out_shape=(
            jax.ShapeDtypeStruct((slots, width + HD), bf16),
            jax.ShapeDtypeStruct((rows, slots), bf16),
        ),
        in_specs=[VM, VM, SM, VM],
        out_specs=(VM, VM),
        name="dispatch",
    )(owners.reshape(1, rows), lengths.reshape(1, rows), counts, queries)


def attend_body(heads, block, recv, keys, values, out, ordered, result, tiles, acc, top):
    width = heads * HD
    slots = recv.shape[0]
    tile_i = jnp.concatenate([recv[:, width:].astype(f32)] * (slots // HD), axis=1)
    tile_j = tile_i.T
    i = lax.broadcasted_iota(i32, (slots, slots), 0)
    j = lax.broadcasted_iota(i32, (slots, slots), 1)
    before = (tile_i > tile_j) | ((tile_i == tile_j) & (i < j))
    rank = jnp.sum(jnp.where(before, 1.0, 0.0), axis=0, keepdims=True)
    rank = jnp.broadcast_to(rank, (slots, slots))
    sort = jnp.where(rank == i.astype(f32), 1.0, 0.0).astype(bf16)
    ordered[...] = jnp.dot(sort, recv[:, :width], preferred_element_type=f32).astype(bf16)
    tile_sorted = jnp.dot(sort, recv[:, width:], preferred_element_type=f32)
    tiles[...] = tile_sorted
    for b in range(slots // block):
        top[b] = jnp.max(tile_sorted[b * block : b * block + 8, :]).astype(i32)
    result[...] = jnp.zeros_like(result)
    cuts = [(o, min(256, TP - o)) for o in range(0, TP, 256)]

    @pl.loop(0, slots // block)
    def _(b):
        count = top[b]

        @pl.when(count > 0)
        def _():
            first = pl.multiple_of(b * block, block)
            rows = ordered[pl.ds(first, block), :]
            query = jnp.concatenate([rows[:, h * HD : (h + 1) * HD] for h in range(heads)], axis=0)
            scaled = query.astype(f32) * HD ** (-0.5)
            high = scaled.astype(bf16)
            low = (scaled - high.astype(f32)).astype(bf16)
            query = jnp.concatenate([high, low], axis=1)
            seen = jnp.concatenate([tiles[pl.ds(first, block), :]] * heads, axis=0)[:, :1]

            def score(t, o, w):
                return jnp.dot(query, keys[t, :, o : o + w], preferred_element_type=f32)

            shift = jnp.max(score(0, 0, 256), axis=1, keepdims=True)
            acc[...] = jnp.zeros_like(acc)

            @pl.loop(0, count)
            def _(t):
                moved = jnp.where(seen > t.astype(f32), shift, HUGE)
                weights = [jnp.exp(score(t, o, w) - moved).astype(bf16) for o, w in cuts]
                acc[...] += jnp.dot(
                    jnp.concatenate(weights, axis=1), values[t], preferred_element_type=f32
                )

            unsafe = jnp.max(jnp.where(acc[:, HD:] < HUGE, 0.0, 1.0))

            @pl.when(unsafe > 0.0)
            def _():
                acc[...] = jnp.zeros_like(acc)

                def step(t, peak):
                    visible = seen > t.astype(f32)
                    scores = jnp.concatenate([score(t, o, w) for o, w in cuts], axis=1)
                    raised = jnp.maximum(peak, jnp.max(scores, axis=1, keepdims=True))
                    raised = jnp.where(visible, raised, peak)
                    weights = jnp.exp(scores - jnp.where(visible, raised, HUGE)).astype(bf16)
                    acc[...] = acc[...] * jnp.exp(peak - raised) + jnp.dot(
                        weights, values[t], preferred_element_type=f32
                    )
                    return raised

                lax.fori_loop(0, count, step, jnp.full((heads * block, 1), -HUGE, f32))

            total = acc[:, HD:]
            mean = acc[:, :HD] / jnp.where(total > 0.0, total, 1.0)
            mean = jnp.where(total > 0.0, mean, 0.0).astype(bf16)
            for h in range(heads):
                result[pl.ds(first, block), h * HD : (h + 1) * HD] = mean[h * block : (h + 1) * block, :]

    unsort = jnp.where(rank.T == j.astype(f32), 1.0, 0.0).astype(bf16)
    out[...] = jnp.dot(unsort, result[...], preferred_element_type=f32).astype(bf16)


def attend(recv, keys, values, block):
    slots = recv.shape[0]
    width = recv.shape[1] - HD
    heads = width // HD
    return pl.pallas_call(
        functools.partial(attend_body, heads, block),
        out_shape=jax.ShapeDtypeStruct((slots, width), bf16),
        in_specs=[VM] * 3,
        out_specs=VM,
        scratch_shapes=[
            pltpu.VMEM((slots, width), bf16),
            pltpu.VMEM((slots, width), bf16),
            pltpu.VMEM((slots, HD), f32),
            pltpu.VMEM((heads * block, 2 * HD), f32),
            pltpu.SMEM((slots // block,), i32),
        ],
        compiler_params=pltpu.CompilerParams(vmem_limit_bytes=50 * 2**20),
        name="attend",
    )(recv, keys, values)


def restore_body(back, returned, out):
    out[...] = jnp.dot(back[...], returned[...], preferred_element_type=f32).astype(bf16)


def restore(back, returned):
    return pl.pallas_call(
        restore_body,
        out_shape=jax.ShapeDtypeStruct((back.shape[0], returned.shape[1]), bf16),
        in_specs=[VM, VM],
        out_specs=VM,
        name="restore",
    )(back, returned)


def project_body(gate, rows, weight, out, acc):
    k = pl.program_id(0)

    @pl.when(k == 0)
    def _():
        acc[...] = jnp.zeros_like(acc)

    acc[...] += jnp.dot(rows[...], weight[...], preferred_element_type=f32)

    @pl.when(k == pl.num_programs(0) - 1)
    def _():
        out[...] = (gate[0] * acc[...]).astype(bf16)


def project(gate, rows, weight):
    count, depth = rows.shape
    width = weight.shape[1]
    step = 1024
    return pl.pallas_call(
        project_body,
        grid=(depth // step,),
        out_shape=jax.ShapeDtypeStruct((count, width), bf16),
        in_specs=[
            SM,
            pl.BlockSpec((count, step), lambda k: (0, k)),
            pl.BlockSpec((step, width), lambda k: (k, 0)),
        ],
        out_specs=pl.BlockSpec((count, width), lambda k: (0, 0)),
        scratch_shapes=[pltpu.VMEM((count, width), f32)],
        compiler_params=pltpu.CompilerParams(vmem_limit_bytes=32 * 2**20),
        name="project",
    )(gate, rows, weight)


def cache_form(img_keys, img_values):
    keys = img_keys[0].reshape(TILES, TILE, HD)
    values = img_values[0].reshape(TILES, TILE, HD)
    keys = jnp.pad(keys, ((0, 0), (0, TP - TILE), (0, 0)), mode="edge").transpose(0, 2, 1)
    keys = jnp.concatenate([keys, keys], axis=1)
    values = jnp.concatenate([values, jnp.ones_like(values)], axis=2)
    values = jnp.pad(values, ((0, 0), (0, TP - TILE), (0, 0)))
    return keys, values


def shards(queries, row_counts, owners, lengths, img_keys, img_values, out_weight, gate_scalar):
    groups = lax.axis_size("grp")
    slots = groups * CAP
    width = queries.shape[1]
    send, back = dispatch(owners, lengths, row_counts, queries, slots)
    keys, values = cache_form(img_keys, img_values)
    recv = lax.all_to_all(send.reshape(groups, CAP, width + HD), "grp", split_axis=0, concat_axis=0, tiled=True)
    result = attend(recv.reshape(slots, width + HD), keys, values, 64)
    returned = lax.all_to_all(result.reshape(groups, CAP, width), "grp", split_axis=0, concat_axis=0, tiled=True)
    rows = restore(back, returned.reshape(slots, width))
    rows = lax.all_gather(rows, "tp", axis=1, tiled=True)
    return project(jnp.tanh(gate_scalar), rows, out_weight)


def solution(mesh):
    placed = (
        P("grp", "tp"),
        P("grp"),
        P("grp"),
        P("grp"),
        P("grp", None, "tp"),
        P("grp", None, "tp"),
        P(None, "tp"),
        P(),
    )
    return jax.shard_map(
        shards, mesh=mesh, in_specs=placed, out_specs=P("grp", "tp"), check_vma=False
    )
```

time: 210 us -> 147 us (0.70); the launches traced: 209 us -> 148 us
  matrix products: 69.3 us -> 0 us
  blocking collectives: 0 us -> 35.3 us
  Pallas kernels: 0 us -> 31.8 us
  waiting for transfers between devices: 63.9 us -> 37.1 us
  other arithmetic: 21.9 us -> 4.23 us
  starting transfers between devices: 17.8 us -> 8.64 us
  local copies, waits for them, and re-layouts: 20.7 us -> 16.2 us
    dot_general x17 -> x0, matrix products: 69.3 us -> none  [the longest x8 40.8 us: attend_block(): jnp.einsum('bkgd,lkd->bkgl', grouped, key_cache, preferred_element_type=j...]
    all_to_all x0 -> x1, blocking collectives: none -> 35.3 us  [shards(): lax.all_to_all(result.reshape(groups, CAP, width), 'grp', split_axis=0, c...]
    pallas_call x0 -> x4, Pallas kernels: none -> 31.8 us  [the longest x1 19.5 us: attend(): pl.pallas_call(functools.partial(attend_body, heads, block), out_shape=ja...]
    all_to_all x3 -> x1, waiting for transfers between devices: 31.6 us -> 4.81 us  [shards(): lax.all_to_all(send.reshape(groups, CAP, width + HD), 'grp', split_axis=0...]
    reduce_sum x9 -> x0, other arithmetic: 15.9 us -> none  [the longest x8 15.2 us: attend_block(): total_weight = jnp.sum(weights, axis=-1)]
    all_to_all x3 -> x1, starting transfers between devices: 17.6 us -> 8.6 us  [shards(): lax.all_to_all(send.reshape(groups, CAP, width + HD), 'grp', split_axis=0...]
    unnamed x0 -> x9, local copies, waits for them, and re-layouts: none -> 7.98 us
    while x32 -> x0, local copies, waits for them, and re-layouts: 7.57 us -> none
  transfers between devices with their start and end apart: 4 -> 2, of which waited for: 4 -> 2; matrix products, arithmetic and copies ran while one was open for 2% -> 8% of each run, Pallas kernels for 0% -> 0%
where the time goes in v1:
time: 147 us; the launch traced here: 148 us
  waiting for transfers between devices  37.1 us (25%)
  blocking collectives  35.3 us (24%)
  Pallas kernels  31.8 us (22%)
  local copies, waits for them, and re-layouts  16.2 us (11%)
  between operations  14.9 us (10%)
  starting transfers between devices  8.64 us (6%)
  other arithmetic  4.23 us (3%)
    all_to_all x1, blocking collectives, shards(): lax.all_to_all(result.reshape(groups, CAP, width), 'grp', split_axis=0, c...  35.3 us
    all_gather x1, waiting for transfers between devices, shards(): rows = lax.all_gather(rows, 'tp', axis=1, tiled=True)  32.3 us
    pallas_call x1, Pallas kernels, attend(): pl.pallas_call(functools.partial(attend_body, heads, block), out_shape=ja...  19.5 us
    all_to_all x1, starting transfers between devices, shards(): lax.all_to_all(send.reshape(groups, CAP, width + HD), 'grp', split_axis=0...  8.6 us
    unnamed x9, local copies, waits for them, and re-layouts  7.98 us
    pallas_call x1, Pallas kernels, project(): pl.pallas_call(project_body, grid=(depth // step,), out_shape=jax.ShapeDt...  7 us
    all_to_all x1, waiting for transfers between devices, shards(): lax.all_to_all(send.reshape(groups, CAP, width + HD), 'grp', split_axis=0...  4.81 us
    another operation x2, local copies, waits for them, and re-layouts, cache_form(): keys = img_keys[0].reshape(TILES, TILE, HD)  4.35 us
  transfers between devices with their start and end apart: 2, of which 2 were waited for; matrix products, arithmetic and copies ran while one was open for 8% of the time, Pallas kernels for 0%

profile of v1, /device:TPU:1, one launch (start us, length us, event | category | flops | bytes accessed | tf_op | source)
XLA Modules:
  0.0 148.2 jit_solution(2257655722445057214)
XLA Ops:
  6.5 0.0 copy-start.3
  7.3 2.8 %dispatch.1 = (bf16[512,1152]{1,0:T(8,128)(2,1)}, bf16[256,512]{1,0:T(8,128)(2,1)}) custom-call(s32[1,256]{1,0:T(1,128)} %bitcast.16, s32[1,256]{1,0:T(1,128)} %bitcast.17, s32[1]{0:T(128)S(6)} %copy.13.counts, bf16[256,1024]{1,0:T(8,128)(2,1)} %queries.1), custom_call_target="tpu_custom_call" | custom-call | tf_op jit(solution)/shard_map/dispatch/pallas_call | solution.py:47
  10.1 8.6 %all-to-all-start = ((bf16[16,32,1152]{2,1,0:T(8,128)(2,1)}), bf16[16,32,1152]{2,1,0:T(8,128)(2,1)S(1)}, u32[]{:S(2)}, u32[]{:S(2)}) async-start(bf16[16,32,1152]{2,1,0:T(8,128)(2,1)} %bitcast.14), calls=%async_computation | async-start | bytes 2359296 | tf_op jit(solution)/shard_map/all_to_all | solution.py:221
  18.7 0.0 all-gather.2.cloned.1.call-start
  18.7 0.0 copy-done.3
  18.7 1.6 %reshape_squeeze.6 = bf16[4,1601,128]{2,1,0:T(8,128)(2,1)} reshape(bf16[1,6404,128]{2,1,0:T(8,128)(2,1)S(1)} %copy-done.3) | data formatting | bytes 3278848 | tf_op jit(solution)/shard_map/reshape;squeeze | solution.py:206
  20.4 2.7 %copy.9 = bf16[4,1601,128]{1,2,0:T(8,128)(2,1)S(1)} copy(bf16[4,1601,128]{2,1,0:T(8,128)(2,1)} %reshape_squeeze.6) | data formatting | bytes 3278848 | tf_op jit(solution)/shard_map/reshape;squeeze | solution.py:206
  23.1 0.7 slice.8
  23.8 3.1 %reshape_squeeze.7 = bf16[4,1601,128]{2,1,0:T(8,128)(2,1)} reshape(bf16[1,6404,128]{2,1,0:T(8,128)(2,1)} %param.13) | data formatting | bytes 3278848 | tf_op jit(solution)/shard_map/reshape;squeeze | solution.py:207
  26.9 0.1 reshape.27
  27.0 0.2 maximum_bitcast_fusion
  27.2 0.0 copy-start.2
  27.2 2.0 %pad_maximum_fusion.keys = bf16[4,256,1664]{2,1,0:T(8,128)(2,1)} fusion(bf16[4,128,1664]{2,1,0:T(8,128)(2,1)S(1)} %maximum_bitcast_fusion), kind=kLoop, calls=%fused_computation.2 | loop fusion | flops 6815744 | bytes 5111808 | tf_op jit(solution)/shard_map/concatenate | solution.py:209
  29.2 0.0 copy-done.2
  29.2 2.1 %fusion.values = bf16[4,1664,256]{2,1,0:T(8,128)(2,1)} fusion(bf16[4,1601,128]{2,1,0:T(8,128)(2,1)S(1)} %copy-done.2), kind=kLoop, calls=%fused_computation.1 | loop fusion | flops 3407872 | bytes 5047296 | tf_op jit(solution)/shard_map/jit(_pad)/pad | solution.py:211
  31.3 4.8 %all-to-all-done = bf16[16,32,1152]{2,1,0:T(8,128)(2,1)S(1)} async-done(((bf16[16,32,1152]{2,1,0:T(8,128)(2,1)}), bf16[16,32,1152]{2,1,0:T(8,128)(2,1)S(1)}, u32[]{:S(2)}, u32[]{:S(2)}) %all-to-all-start) | async-done | bytes 1179680 | tf_op jit(solution)/shard_map/all_to_all | solution.py:221
  36.1 19.5 %attend.1 = bf16[512,1024]{1,0:T(8,128)(2,1)S(1)} custom-call(bf16[512,1152]{1,0:T(8,128)(2,1)S(1)} %bitcast.11, bf16[4,256,1664]{2,1,0:T(8,128)(2,1)} %pad_maximum_fusion.keys, bf16[4,1664,256]{2,1,0:T(8,128)(2,1)} %fusion.values), custom_call_target="tpu_custom_call" | custom-call | tf_op jit(solution)/shard_map/attend/pallas_call | solution.py:140
  55.6 35.3 %all_to_all.10 = bf16[16,32,1024]{2,1,0:T(8,128)(2,1)} all-to-all(bf16[16,32,1024]{2,1,0:T(8,128)(2,1)S(1)} %bitcast.12), channel_id=1, replica_groups=mesh['grp'=16,'tp'=8] {'grp'}, dimensions={0} | all-to-all | bytes 2097152 | tf_op jit(solution)/shard_map/all_to_all | solution.py:223
  90.9 2.5 %restore.1 = bf16[256,1024]{1,0:T(8,128)(2,1)} custom-call(bf16[256,512]{1,0:T(8,128)(2,1)} %get-tuple-element.7.back, bf16[512,1024]{1,0:T(8,128)(2,1)} %bitcast.13), custom_call_target="tpu_custom_call" | custom-call | tf_op jit(solution)/shard_map/restore/pallas_call | solution.py:162
  93.4 0.0 all-gather.2.cloned.1.call-update
  94.1 32.3 %all-gather.2.cloned.1.call-done.rows = bf16[256,8192]{1,0:T(8,128)(2,1)} async-done(((bf16[256,1024]{1,0:T(8,128)(2,1)}), bf16[256,8192]{1,0:T(8,128)(2,1)}) %all-gather.2.cloned.1.call-update) | async-done | bytes 4194320 | tf_op jit(solution)/shard_map/all_gather | solution.py:225
  126.4 0.0 copy-start
  126.4 5.8 %copy-done = bf16[8192,1024]{1,0:T(8,128)(2,1)S(1)} copy-done((bf16[8192,1024]{1,0:T(8,128)(2,1)S(1)}, bf16[8192,1024]{1,0:T(8,128)(2,1)}, u32[]{:S(2)}) %copy-start) | copy-done | bytes 16777240
  132.1 0.0 copy-start.1
  132.1 2.2 %copy-done.1 = bf16[256,8192]{1,0:T(8,128)(2,1)S(1)} copy-done((bf16[256,8192]{1,0:T(8,128)(2,1)S(1)}, bf16[256,8192]{1,0:T(8,128)(2,1)}, u32[]{:S(2)}) %copy-start.1) | copy-done | bytes 4194328
  134.3 7.0 %project.1 = bf16[256,1024]{1,0:T(8,128)(2,1)} custom-call(f32[1]{0:T(128)S(6)} %tanh.3.gate, bf16[256,8192]{1,0:T(8,128)(2,1)S(1)} %copy-done.1, bf16[8192,1024]{1,0:T(8,128)(2,1)S(1)} %copy-done), custom_call_target="tpu_custom_call" | custom-call | tf_op jit(solution)/shard_map/project/pallas_call | solution.py:189
  (1 shorter events, 0.0 us)
Async XLA Ops:
  6.5 12.2 %copy-start.3 = (bf16[1,6404,128]{2,1,0:T(8,128)(2,1)S(1)}, bf16[1,6404,128]{2,1,0:T(8,128)(2,1)}, u32[]{:S(2)}) copy-start(bf16[1,6404,128]{2,1,0:T(8,128)(2,1)} %param.12) | copy-start | bytes 4918276
  10.1 26.0 %all-to-all-start = ((bf16[16,32,1152]{2,1,0:T(8,128)(2,1)}), bf16[16,32,1152]{2,1,0:T(8,128)(2,1)S(1)}, u32[]{:S(2)}, u32[]{:S(2)}) async-start(bf16[16,32,1152]{2,1,0:T(8,128)(2,1)} %bitcast.14), calls=%async_computation | async-start | bytes 2359296 | tf_op jit(solution)/shard_map/all_to_all | solution.py:221
  18.7 107.7 %all-gather.2.cloned.1.call-start = ((), (), s32[]{:S(2)}) async-start(), calls=%async_computation.2 | async-start | bytes 4718592 | tf_op jit(solution)/shard_map/all_gather | solution.py:225
  27.2 2.0 %copy-start.2 = (bf16[4,1601,128]{2,1,0:T(8,128)(2,1)S(1)}, bf16[4,1601,128]{2,1,0:T(8,128)(2,1)}, u32[]{:S(2)}) copy-start(bf16[4,1601,128]{2,1,0:T(8,128)(2,1)} %reshape_squeeze.7) | copy-start | bytes 4918276
  126.4 5.8 %copy-start = (bf16[8192,1024]{1,0:T(8,128)(2,1)S(1)}, bf16[8192,1024]{1,0:T(8,128)(2,1)}, u32[]{:S(2)}) copy-start(bf16[8192,1024]{1,0:T(8,128)(2,1)} %weight.1) | copy-start | bytes 50331652
  132.1 2.2 %copy-start.1 = (bf16[256,8192]{1,0:T(8,128)(2,1)S(1)}, bf16[256,8192]{1,0:T(8,128)(2,1)}, u32[]{:S(2)}) copy-start(bf16[256,8192]{1,0:T(8,128)(2,1)} %all-gather.2.cloned.1.call-done.rows) | copy-start | bytes 12582916
Sparse Core Ops, SparseCore 0:
  93.6 32.7 all-gather.1

commit v2 on v1

v2 whole, which is shorter than its diff:
```python
import functools

import jax
import jax.numpy as jnp
from jax import lax
from jax.experimental import pallas as pl
from jax.experimental.pallas import tpu as pltpu
from jax.sharding import PartitionSpec as P

f32, bf16, i32 = jnp.float32, jnp.bfloat16, jnp.int32
HD = 128
CAP = 32
TILE = 1601
TILES = 4
TP = 1664
VR = 144
LOG2E = 1.4426950408889634
BLOCK = 128
CUTS = [(o, min(256, TP - o)) for o in range(0, TP, 256)]
HUGE = 1e30
UNROLL = 1
VM = pl.BlockSpec(memory_space=pltpu.VMEM)
SM = pl.BlockSpec(memory_space=pltpu.SMEM)
HB = pl.BlockSpec(memory_space=pltpu.HBM)


def like(shape, kind):
    return jax.ShapeDtypeStruct(shape, kind)


def near(x):
    return pltpu.with_memory_space_constraint(x, pltpu.VMEM)


def far(x):
    return pltpu.with_memory_space_constraint(x, pltpu.HBM)


def dispatch_body(owners, lengths, counts, queries, send, place):
    rows = queries.shape[0]
    slots = send.shape[0]
    width = queries.shape[1]
    i = lax.broadcasted_iota(i32, (rows, rows), 0)
    j = lax.broadcasted_iota(i32, (rows, rows), 1)
    own_j = jnp.broadcast_to(owners[...].astype(f32), (rows, rows))
    same = (own_j.T == own_j) & (i < j) & (i < counts[0])
    pos = jnp.sum(jnp.where(same, 1.0, 0.0), axis=0, keepdims=True)
    live = lax.broadcasted_iota(i32, (1, rows), 1) < counts[0]
    target = jnp.where(live, owners[...].astype(f32) * CAP + pos, -1.0)
    slot = lax.broadcasted_iota(i32, (slots, rows), 0).astype(f32)
    pick = jnp.where(jnp.broadcast_to(target, (slots, rows)) == slot, 1.0, 0.0).astype(bf16)
    send[:, :width] = jnp.dot(pick, queries[...], preferred_element_type=f32).astype(bf16)
    seen = sum(jnp.where(lengths[...] > k * TILE, 1.0, 0.0) for k in range(TILES))
    seen = jnp.broadcast_to(seen, (HD, rows)).T.astype(bf16)
    send[:, width:] = jnp.dot(pick, seen, preferred_element_type=f32).astype(bf16)
    place[...] = jnp.broadcast_to(target, place.shape)


def dispatch(owners, lengths, counts, queries, slots):
    rows, width = queries.shape
    return pl.pallas_call(
        dispatch_body,
        out_shape=[like((slots, width + HD), bf16), pltpu.VMEM((8, rows), f32)],
        in_specs=[VM, VM, SM, VM],
        out_specs=[VM, VM],
        name="dispatch",
    )(owners.reshape(1, rows), lengths.reshape(1, rows), counts, queries)


def cache_body(place, img_keys, img_values, keys, values, back):
    total = img_keys.shape[1]
    row = lax.broadcasted_iota(i32, (TP, HD), 0)
    ones = jnp.where(lax.broadcasted_iota(i32, (VR - HD, TP), 1) < TILE, 1.0, 0.0).astype(bf16)
    for source, is_key in ((img_keys, True), (img_values, False)):
        for t in range(TILES):
            first = t * TILE
            low = first // 16 * 16
            high = min(total, -(-(first + TILE) // 16) * 16)
            x = source[0, low:high, :].astype(f32)
            x = jnp.concatenate([x, jnp.zeros((TP + 16 - (high - low), HD), f32)], axis=0)
            if first != low:
                x = pltpu.roll(x, TP + 16 - (first - low), 0)
            x = x[:TP]
            if is_key:
                x = jnp.where(row < TILE, x, jnp.broadcast_to(x[:1], (TP, HD))) * (LOG2E * HD ** (-0.5))
                high_part = x.astype(bf16)
                keys[t, :, :HD] = high_part
                keys[t, :, HD:] = (x - high_part.astype(f32)).astype(bf16)
            else:
                values[t, :HD, :] = jnp.where(row < TILE, x, 0.0).astype(bf16).T
                values[t, HD:, :] = ones
    rows, slots = back.shape
    target = jnp.broadcast_to(place[:1, :], (HD, rows)).T
    lane = lax.broadcasted_iota(i32, (rows, HD), 1).astype(f32)
    for k in range(slots // HD):
        back[:, k * HD : (k + 1) * HD] = jnp.where(target == lane + k * HD, 1.0, 0.0).astype(bf16)


def cache(place, img_keys, img_values, slots):
    return pl.pallas_call(
        cache_body,
        out_shape=[
            like((TILES, TP, 2 * HD), bf16),
            like((TILES, VR, TP), bf16),
            pltpu.VMEM((place.shape[1], slots), bf16),
        ],
        in_specs=[VM, VM, VM],
        out_specs=[VM] * 3,
        compiler_params=pltpu.CompilerParams(vmem_limit_bytes=32 * 2**20),
        name="cache",
    )(near(place), img_keys, img_values)


def attend_body(heads, recv, keys_far, values_far, out, *scratch):
    keys, values, order, blocked, turned, seen, shift, acc, item_b, item_t, sems = scratch
    fetch_keys = pltpu.make_async_copy(keys_far, keys, sems.at[0])
    fetch_values = pltpu.make_async_copy(values_far, values, sems.at[1])
    fetch_keys.start()
    fetch_values.start()
    slots = recv.shape[0]
    width = heads * HD
    blocks = slots // BLOCK
    lanes = heads * BLOCK
    tile_i = jnp.concatenate([recv[:, width:].astype(f32)] * (slots // HD), axis=1)
    tile_j = tile_i.T
    i = lax.broadcasted_iota(i32, (slots, slots), 0)
    j = lax.broadcasted_iota(i32, (slots, slots), 1)
    before = (tile_j > tile_i) | ((tile_j == tile_i) & (j < i))
    rank = jnp.sum(jnp.where(before, 1.0, 0.0), axis=1, keepdims=True)
    placed = rank == j.astype(f32)
    order[...] = jnp.where(placed, 1.0, 0.0).astype(bf16)
    sorted_tiles = jnp.sum(jnp.where(placed, tile_i, 0.0), axis=0, keepdims=True)
    columns = lax.dot_general(
        recv[:, :width], order[...], (((0,), (0,)), ((), ())), preferred_element_type=f32
    ).astype(bf16)
    count = jnp.int32(0)
    for b in range(blocks):
        mine = sorted_tiles[:, b * BLOCK : (b + 1) * BLOCK]
        for h in range(heads):
            x = columns[h * HD : (h + 1) * HD, b * BLOCK : (b + 1) * BLOCK]
            blocked[b, :HD, h * BLOCK : (h + 1) * BLOCK] = x
            blocked[b, HD:, h * BLOCK : (h + 1) * BLOCK] = x
        seen[b] = jnp.broadcast_to(jnp.concatenate([mine] * heads, axis=1), (8, lanes))
        most = jnp.max(mine).astype(i32)
        for t in range(TILES):
            item_b[count] = b
            item_t[count] = t
            count = count + jnp.where(t < most, 1, 0)
    for u in range(UNROLL):
        item_b[count + u] = 0
        item_t[count + u] = TILES
    acc[...] = jnp.zeros_like(acc)

    def score(t, o, w, query):
        return jnp.dot(keys[t, o : o + w, :], query, preferred_element_type=f32)

    fetch_keys.wait()

    @pl.loop(0, blocks)
    def _(b):
        peak = jnp.max(score(0, 0, 256, blocked[b]), axis=0, keepdims=True)
        shift[b] = jnp.broadcast_to(peak, (8, lanes))

    fetch_values.wait()

    def work(b, t):
        tile = jnp.minimum(t, TILES - 1)
        query = blocked[b]
        moved = jnp.where(seen[b, :1, :] > t.astype(f32), shift[b, :1, :], HUGE)
        weights = [jnp.exp2(score(tile, o, w, query) - moved).astype(bf16) for o, w in CUTS]
        acc[b] += jnp.dot(values[tile], jnp.concatenate(weights, axis=0), preferred_element_type=f32)

    @pl.loop(0, (count + UNROLL - 1) // UNROLL)
    def _(n):
        for u in range(UNROLL):
            work(item_b[UNROLL * n + u], item_t[UNROLL * n + u])

    unsafe = jnp.max(jnp.where(acc[:, HD : HD + 1, :] < HUGE, 0.0, 1.0))

    @pl.when(unsafe > 0.0)
    def _():
        acc[...] = jnp.zeros_like(acc)
        shift[...] = jnp.full(shift.shape, -HUGE, f32)

        @pl.loop(0, count)
        def _(n):
            b, t = item_b[n], item_t[n]
            query = blocked[b]
            visible = seen[b, :1, :] > t.astype(f32)
            peak = shift[b, :1, :]
            scores = jnp.concatenate([score(t, o, w, query) for o, w in CUTS], axis=0)
            raised = jnp.where(visible, jnp.maximum(peak, jnp.max(scores, axis=0, keepdims=True)), peak)
            weights = jnp.exp2(scores - jnp.where(visible, raised, HUGE)).astype(bf16)
            acc[b] = acc[b] * jnp.exp2(peak - raised) + jnp.dot(
                values[t], weights, preferred_element_type=f32
            )
            shift[b] = jnp.broadcast_to(raised, (8, lanes))

    for b in range(blocks):
        total = acc[b, HD : HD + 1, :]
        inverse = jnp.where(total > 0.0, 1.0 / jnp.where(total > 0.0, total, 1.0), 0.0)
        mean = (acc[b, :HD, :] * inverse).astype(bf16)
        for h in range(heads):
            turned[h * HD : (h + 1) * HD, b * BLOCK : (b + 1) * BLOCK] = mean[
                :, h * BLOCK : (h + 1) * BLOCK
            ]
    out[...] = lax.dot_general(
        order[...], turned[...], (((1,), (1,)), ((), ())), preferred_element_type=f32
    ).astype(bf16)


def attend(recv, keys, values):
    slots = recv.shape[0]
    width = recv.shape[1] - HD
    heads = width // HD
    blocks = slots // BLOCK
    lanes = heads * BLOCK
    return pl.pallas_call(
        functools.partial(attend_body, heads),
        out_shape=like((slots, width), bf16),
        in_specs=[VM, HB, HB],
        out_specs=VM,
        scratch_shapes=[
            pltpu.VMEM(keys.shape, bf16),
            pltpu.VMEM(values.shape, bf16),
            pltpu.VMEM((slots, slots), bf16),
            pltpu.VMEM((blocks, 2 * HD, lanes), bf16),
            pltpu.VMEM((width, slots), bf16),
            pltpu.VMEM((blocks, 8, lanes), f32),
            pltpu.VMEM((blocks, 8, lanes), f32),
            pltpu.VMEM((blocks, VR, lanes), f32),
            pltpu.SMEM((blocks * TILES + UNROLL,), i32),
            pltpu.SMEM((blocks * TILES + UNROLL,), i32),
            pltpu.SemaphoreType.DMA((2,)),
        ],
        compiler_params=pltpu.CompilerParams(vmem_limit_bytes=42 * 2**20),
        cost_estimate=pl.CostEstimate(
            flops=4 * slots * heads * TP * TILES * HD,
            bytes_accessed=8 * 2**20,
            transcendentals=slots * heads * TP * TILES,
        ),
        name="attend",
    )(recv, far(keys), far(values))


def restore_body(back, returned, upper, lower):
    rows = jnp.dot(back[...], returned[...], preferred_element_type=f32).astype(bf16)
    half = upper.shape[0]
    upper[...] = rows[:half]
    lower[...] = rows[half:]


def restore(back, returned):
    rows, width = back.shape[0], returned.shape[1]
    return pl.pallas_call(
        restore_body,
        out_shape=[like((rows // 2, width), bf16)] * 2,
        in_specs=[VM, VM],
        out_specs=[VM, VM],
        name="restore",
    )(near(back), returned)


def project_body(count, first, last, starts, gate, weight, *refs):
    pieces = refs[: 2 * count]
    before = None if first else refs[2 * count]
    out, held, rows, sems = refs[-4:]
    half, depth = pieces[0].shape

    def fetch(n):
        start = pl.multiple_of(starts[n], depth)
        return [
            pltpu.make_async_copy(weight.at[pl.ds(start, depth), :], held.at[n], sems.at[3 * n]),
            pltpu.make_async_copy(pieces[2 * n], rows.at[n, pl.ds(0, half), :], sems.at[3 * n + 1]),
            pltpu.make_async_copy(pieces[2 * n + 1], rows.at[n, pl.ds(half, half), :], sems.at[3 * n + 2]),
        ]

    for n in range(count):
        for copy in fetch(n):
            copy.start()
    total = None if first else before[...]
    for n in range(count):
        for copy in fetch(n):
            copy.wait()
        term = jnp.dot(rows[n], held[n], preferred_element_type=f32)
        total = term if total is None else total + term
    out[...] = (gate[0] * total).astype(bf16) if last else total


def project(starts, gate, weight, pieces, before, last):
    count = len(pieces)
    half, depth = pieces[0][0].shape
    width = weight.shape[1]
    given = [jnp.stack(starts).astype(i32), gate, far(weight)]
    given += [far(x) for pair in pieces for x in pair]
    spaces = [SM, SM] + [HB] * (1 + 2 * count)
    if before is not None:
        given.append(near(before))
        spaces.append(VM)
    return pl.pallas_call(
        functools.partial(project_body, count, before is None, last),
        out_shape=like((2 * half, width), bf16) if last else pltpu.VMEM((2 * half, width), f32),
        in_specs=spaces,
        out_specs=VM,
        scratch_shapes=[
            pltpu.VMEM((count, depth, width), bf16),
            pltpu.VMEM((count, 2 * half, depth), bf16),
            pltpu.SemaphoreType.DMA((3 * count,)),
        ],
        compiler_params=pltpu.CompilerParams(vmem_limit_bytes=32 * 2**20),
        name="project",
    )(*given)


def shards(queries, row_counts, owners, lengths, img_keys, img_values, out_weight, gate_scalar):
    groups = lax.axis_size("grp")
    shares = lax.axis_size("tp")
    chips = shares // 2
    slots = groups * CAP
    width = queries.shape[1]
    me = lax.axis_index("tp")
    gate = jnp.tanh(gate_scalar)

    def exchange(x):
        x = x.reshape(groups, CAP, x.shape[1])
        x = lax.all_to_all(x, "grp", split_axis=0, concat_axis=0, tiled=True)
        return x.reshape(slots, x.shape[2])

    def round_chips(x, by):
        return lax.ppermute(x, "tp", [(d, (d + 2 * by) % shares) for d in range(shares)])

    def other_core(x):
        return lax.ppermute(x, "tp", [(d, d ^ 1) for d in range(shares)])

    def start(by, core):
        share = (me - 2 * by) % shares
        return (share ^ core) * width

    def both(pair):
        return [other_core(x) for x in pair]

    send, place = dispatch(owners, lengths, row_counts, queries, slots)
    received = exchange(send)
    keys, values, back = cache(place, img_keys, img_values, slots)
    upper, lower = restore(back, exchange(attend(received, keys, values)))
    back_by = chips - 1
    left_upper, right_lower = round_chips(upper, 1), round_chips(lower, back_by)
    left_lower, right_upper = round_chips(lower, 1), round_chips(upper, back_by)
    across = [round_chips(left_upper, 1), round_chips(right_lower, back_by)]
    own = [upper, lower]
    total = project([start(0, 0), start(0, 1)], gate, out_weight, [own, both(own)], None, False)
    left, right = [left_upper, left_lower], [right_upper, right_lower]
    left, right, total = lax.optimization_barrier((left, right, total))
    total = project(
        [start(1, 0), start(-1, 0), start(1, 1), start(-1, 1)],
        gate,
        out_weight,
        [left, right, both(left), both(right)],
        total,
        False,
    )
    across, total = lax.optimization_barrier((across, total))
    beside = both(across)
    total = project([start(2, 0)], gate, out_weight, [across], total, False)
    return project([start(2, 1)], gate, out_weight, [beside], total, True)


def solution(mesh):
    placed = (
        P("grp", "tp"),
        P("grp"),
        P("grp"),
        P("grp"),
        P("grp", None, "tp"),
        P("grp", None, "tp"),
        P(None, "tp"),
        P(),
    )
    return jax.shard_map(
        shards, mesh=mesh, in_specs=placed, out_specs=P("grp", "tp"), check_vma=False
    )
```

time: 147 us -> 115 us (0.78)
  waiting for transfers between devices: 37.1 us -> 16.9 us
  between operations: 14.9 us -> 1.84 us
  starting transfers between devices: 8.64 us -> 21.6 us
  local copies, waits for them, and re-layouts: 16.2 us -> 7.33 us
  Pallas kernels: 31.8 us -> 37.3 us
  other arithmetic: 4.23 us -> 0.15 us
  blocking collectives: 35.3 us -> 31.5 us
    all_gather x1 -> x0, waiting for transfers between devices: 32.3 us -> none  [shards(): rows = lax.all_gather(rows, 'tp', axis=1, tiled=True)]
    ppermute x0 -> x14, starting transfers between devices: none -> 13 us  [the longest x6 7.53 us: round_chips(): lax.ppermute(x, 'tp', [(d, (d + 2 * by) % shares) for d in range(shares)])]
    another operation x3 -> x0, local copies, waits for them, and re-layouts: 7.41 us -> none  [the longest x2 4.35 us: cache_form(): keys = img_keys[0].reshape(TILES, TILE, HD)]
    all_to_all x1, waiting for transfers between devices: 4.81 us -> 11 us  [exchange(): x = lax.all_to_all(x, 'grp', split_axis=0, concat_axis=0, tiled=True)]
    ppermute x0 -> x14, waiting for transfers between devices: none -> 5.91 us  [the longest x6 5.34 us: round_chips(): lax.ppermute(x, 'tp', [(d, (d + 2 * by) % shares) for d in range(shares)])]
    pallas_call x4 -> x8, Pallas kernels: 31.8 us -> 37.3 us  [the longest x4 15.2 us: project(): pl.pallas_call(functools.partial(project_body, count, before is None, las...]
    all_to_all x1, blocking collectives: 35.3 us -> 31.5 us  [exchange(): x = lax.all_to_all(x, 'grp', split_axis=0, concat_axis=0, tiled=True)]
    pad x1 -> x0, other arithmetic: 2.09 us -> none  [cache_form(): values = jnp.pad(values, ((0, 0), (0, TP - TILE), (0, 0)))]
  transfers between devices with their start and end apart: 2 -> 15, of which waited for: 2 -> 3; matrix products, arithmetic and copies ran while one was open for 8% -> 0% of each run, Pallas kernels for 0% -> 12%
where the time goes in v2:
time: 115 us; the launch traced here: 117 us
  Pallas kernels  37.3 us (32%)
  blocking collectives  31.5 us (27%)
  starting transfers between devices  21.6 us (19%)
  waiting for transfers between devices  16.9 us (15%)
  local copies, waits for them, and re-layouts  7.33 us (6%)
  between operations  1.84 us (2%)
    all_to_all x1, blocking collectives, exchange(): x = lax.all_to_all(x, 'grp', split_axis=0, concat_axis=0, tiled=True)  31.5 us
    pallas_call x4, Pallas kernels, project(): pl.pallas_call(functools.partial(project_body, count, before is None, las...  15.2 us
    pallas_call x1, Pallas kernels, attend(): pl.pallas_call(functools.partial(attend_body, heads), out_shape=like((slo...  15 us
    all_to_all x1, waiting for transfers between devices, exchange(): x = lax.all_to_all(x, 'grp', split_axis=0, concat_axis=0, tiled=True)  11 us
    all_to_all x1, starting transfers between devices, exchange(): x = lax.all_to_all(x, 'grp', split_axis=0, concat_axis=0, tiled=True)  8.6 us
    ppermute x6, starting transfers between devices, round_chips(): lax.ppermute(x, 'tp', [(d, (d + 2 * by) % shares) for d in range(shares)])  7.53 us
    unnamed x32, local copies, waits for them, and re-layouts  7.33 us
    ppermute x8, starting transfers between devices, other_core(): return lax.ppermute(x, 'tp', [(d, d ^ 1) for d in range(shares)])  5.48 us
  transfers between devices with their start and end apart: 15, of which 3 were waited for; matrix products, arithmetic and copies ran while one was open for 0% of the time, Pallas kernels for 12%

profile of v2, /device:TPU:1, one launch (start us, length us, event | category | flops | bytes accessed | tf_op | source)
XLA Modules:
  0.0 116.6 jit_solution(14850042271527367581)
XLA Ops:
  0.8 2.7 %dispatch.1 = (bf16[512,1152]{1,0:T(8,128)(2,1)}, f32[8,256]{1,0:T(8,128)S(1)}) custom-call(s32[1,256]{1,0:T(1,128)} %bitcast.18, s32[1,256]{1,0:T(1,128)} %bitcast.19, s32[1]{0:T(128)S(6)} %copy.9.counts, bf16[256,1024]{1,0:T(8,128)(2,1)} %queries.1), custom_call_target="tpu_custom_call" | custom-call | tf_op jit(solution)/shard_map/dispatch/pallas_call | solution.py:61
  3.5 8.6 %all-to-all-start = ((bf16[16,32,1152]{2,1,0:T(8,128)(2,1)}), bf16[16,32,1152]{2,1,0:T(8,128)(2,1)S(1)}, u32[]{:S(2)}, u32[]{:S(2)}) async-start(bf16[16,32,1152]{2,1,0:T(8,128)(2,1)} %bitcast.17), calls=%async_computation | async-start | bytes 2359296 | tf_op jit(solution)/shard_map/all_to_all | solution.py:326
  12.1 1.4 %copy-done.1 = bf16[1,6404,128]{2,1,0:T(8,128)(2,1)S(1)} copy-done((bf16[1,6404,128]{2,1,0:T(8,128)(2,1)S(1)}, bf16[1,6404,128]{2,1,0:T(8,128)(2,1)}, u32[]{:S(2)}) %copy-start.1) | copy-done | bytes 1639448
  13.5 2.0 %cache.1 = (bf16[4,1664,256]{2,1,0:T(8,128)(2,1)S(1)}, bf16[4,144,1664]{2,1,0:T(8,128)(2,1)S(1)}, bf16[256,512]{1,0:T(8,128)(2,1)S(1)}) custom-call(f32[8,256]{1,0:T(8,128)S(1)} %get-tuple-element.20.place, bf16[1,6404,128]{2,1,0:T(8,128)(2,1)S(1)} %copy-done, bf16[1,6404,128]{2,1,0:T(8,128)(2,1)S(1)} %copy-done.1), custom_call_target="tpu_custom_call" | custom-call | tf_op jit(solution)/shard_map/cache/pallas_call | solution.py:100
  15.5 1.7 %copy-done.2 = bf16[4,1664,256]{2,1,0:T(8,128)(2,1)} copy-done((bf16[4,1664,256]{2,1,0:T(8,128)(2,1)}, bf16[4,1664,256]{2,1,0:T(8,128)(2,1)S(1)}, u32[]{:S(2)}) %copy-start.2) | copy-done | bytes 3407896
  17.2 1.3 %copy-done.3 = bf16[4,144,1664]{2,1,0:T(8,128)(2,1)} copy-done((bf16[4,144,1664]{2,1,0:T(8,128)(2,1)}, bf16[4,144,1664]{2,1,0:T(8,128)(2,1)S(1)}, u32[]{:S(2)}) %copy-start.3) | copy-done | bytes 1916952
  18.5 11.0 %all-to-all-done = bf16[16,32,1152]{2,1,0:T(8,128)(2,1)S(1)} async-done(((bf16[16,32,1152]{2,1,0:T(8,128)(2,1)}), bf16[16,32,1152]{2,1,0:T(8,128)(2,1)S(1)}, u32[]{:S(2)}, u32[]{:S(2)}) %all-to-all-start) | async-done | bytes 1179680 | tf_op jit(solution)/shard_map/all_to_all | solution.py:326
  29.5 15.0 %attend.1 = bf16[512,1024]{1,0:T(8,128)(2,1)S(1)} custom-call(bf16[512,1152]{1,0:T(8,128)(2,1)S(1)} %bitcast.14, bf16[4,1664,256]{2,1,0:T(8,128)(2,1)} %copy-done.2, bf16[4,144,1664]{2,1,0:T(8,128)(2,1)} %copy-done.3), custom_call_target="tpu_custom_call" | custom-call | flops 13958643712 | bytes 8388608 | tf_op jit(solution)/shard_map/attend/pallas_call | solution.py:218
  44.5 31.5 %all_to_all.10 = bf16[16,32,1024]{2,1,0:T(8,128)(2,1)} all-to-all(bf16[16,32,1024]{2,1,0:T(8,128)(2,1)S(1)} %bitcast.15), channel_id=1, replica_groups=mesh['grp'=16,'tp'=8] {'grp'}, dimensions={0} | all-to-all | bytes 2097152 | tf_op jit(solution)/shard_map/all_to_all | solution.py:326
  76.0 2.4 %restore.1 = (bf16[128,1024]{1,0:T(8,128)(2,1)}, bf16[128,1024]{1,0:T(8,128)(2,1)}) custom-call(bf16[256,512]{1,0:T(8,128)(2,1)S(1)} %get-tuple-element.21.back, bf16[512,1024]{1,0:T(8,128)(2,1)} %bitcast.16), custom_call_target="tpu_custom_call" | custom-call | tf_op jit(solution)/shard_map/restore/pallas_call | solution.py:255
  78.4 2.0 %collective-permute-start.6 = (bf16[128,1024]{1,0:T(8,128)(2,1)}, bf16[128,1024]{1,0:T(8,128)(2,1)S(1)}, u32[]{:S(2)}, u32[]{:S(2)}) collective-permute-start(bf16[128,1024]{1,0:T(8,128)(2,1)} %get-tuple-element.25.refs_0_), channel_id=1, source_target_pairs={{0,1},{1,0},{2,3},{3,2},{4,5},{5,4},{6,7},{7,6},{8,9},{9,8},{10,11... | collective-permute-start | bytes 786440 | tf_op jit(solution)/shard_map/ppermute | solution.py:333
  80.4 2.5 %collective-permute-start.5 = (bf16[128,1024]{1,0:T(8,128)(2,1)}, bf16[128,1024]{1,0:T(8,128)(2,1)S(1)}, u32[]{:S(2)}, u32[]{:S(2)}) collective-permute-start(bf16[128,1024]{1,0:T(8,128)(2,1)} %get-tuple-element.25.refs_0_), channel_id=1, source_target_pairs={{0,6},{1,7},{2,0},{3,1},{4,2},{5,3},{6,4},{7,5},{8,14},{9,15},{10,... | collective-permute-start | bytes 786440 | tf_op jit(solution)/shard_map/ppermute | solution.py:330
  82.9 0.2 collective-permute-start.4
  83.1 2.7 %collective-permute-start.2 = (bf16[128,1024]{1,0:T(8,128)(2,1)}, bf16[128,1024]{1,0:T(8,128)(2,1)S(1)}, u32[]{:S(2)}, u32[]{:S(2)}) collective-permute-start(bf16[128,1024]{1,0:T(8,128)(2,1)} %get-tuple-element.26.refs_1_), channel_id=1, source_target_pairs={{0,6},{1,7},{2,0},{3,1},{4,2},{5,3},{6,4},{7,5},{8,14},{9,15},{10,... | collective-permute-start | bytes 786440 | tf_op jit(solution)/shard_map/ppermute | solution.py:330
  86.6 0.7 copy-done.13
  87.3 4.3 %project.4.refs_8_ = f32[256,1024]{1,0:T(8,128)S(1)} custom-call(s32[2]{0:T(128)S(1)} %pad_add_fusion.1.starts, f32[1]{0:T(128)S(6)} %tanh.3.gate, bf16[8192,1024]{1,0:T(8,128)(2,1)} %weight.7, bf16[128,1024]{1,0:T(8,128)(2,1)} %get-tuple-element.25.refs_0_, bf16[128,1024]{1,0:T(8,128)(2,1)} %get-tuple-element.26.refs_1_, bf16[128,1024]{1,0:T(8,128)(2,1)} %copy-done.12, ...), custom_call_target="tpu_custom_call" | custom-call | tf_op jit(solution)/shard_map/project/pallas_call | solution.py:300
  91.6 5.3 %collective-permute-done.4.refs_1_ = bf16[128,1024]{1,0:T(8,128)(2,1)S(1)} collective-permute-done((bf16[128,1024]{1,0:T(8,128)(2,1)}, bf16[128,1024]{1,0:T(8,128)(2,1)S(1)}, u32[]{:S(2)}, u32[]{:S(2)}) %collective-permute-start.4) | collective-permute-done | bytes 262176 | tf_op jit(solution)/shard_map/ppermute | solution.py:330
  96.9 1.8 %collective-permute-start.8 = (bf16[128,1024]{1,0:T(8,128)(2,1)S(1)}, bf16[128,1024]{1,0:T(8,128)(2,1)S(1)}, u32[]{:S(2)}, u32[]{:S(2)}) collective-permute-start(bf16[128,1024]{1,0:T(8,128)(2,1)S(1)} %collective-permute-done.refs_0_), channel_id=1, source_target_pairs={{0,1},{1,0},{2,3},{3,2},{4,5},{5,4},{6,7},{7,6},{8,9},{9,8},{10,11... | collective-permute-start | bytes 786440 | tf_op jit(solution)/shard_map/ppermute | solution.py:333
  98.7 0.1 collective-permute-start.9
  98.8 0.4 collective-permute-start.10
  99.2 0.1 collective-permute-start.11
  99.3 0.6 collective-permute-done.8.refs_4_
  99.9 2.1 %collective-permute-start.3 = (bf16[128,1024]{1,0:T(8,128)(2,1)S(1)}, bf16[128,1024]{1,0:T(8,128)(2,1)}, u32[]{:S(2)}, u32[]{:S(2)}) collective-permute-start(bf16[128,1024]{1,0:T(8,128)(2,1)S(1)} %collective-permute-done.2.refs_3_), channel_id=1, source_target_pairs={{0,6},{1,7},{2,0},{3,1},{4,2},{5,3},{6,4},{7,5},{8,14},{9,15},{10,... | collective-permute-start | bytes 786440 | tf_op jit(solution)/shard_map/ppermute | solution.py:330
  102.1 0.7 copy-done.10
  102.8 0.7 copy-done.11
  103.5 5.3 %project.5.refs_2_ = f32[256,1024]{1,0:T(8,128)S(1)} custom-call(s32[4]{0:T(128)S(1)} %pad_add_fusion.starts, f32[1]{0:T(128)S(6)} %tanh.3.gate, bf16[8192,1024]{1,0:T(8,128)(2,1)} %weight.7, bf16[128,1024]{1,0:T(8,128)(2,1)} %copy-done.4, bf16[128,1024]{1,0:T(8,128)(2,1)} %copy-done.7, bf16[128,1024]{1,0:T(8,128)(2,1)} %copy-done.5, ...), custom_call_target="tpu_custom_call" | custom-call | tf_op jit(solution)/shard_map/project/pallas_call | solution.py:300
  108.9 1.1 collective-permute-start.12
  109.9 0.1 collective-permute-start.13
  110.0 2.4 %project.6.refs_2_ = f32[256,1024]{1,0:T(8,128)S(1)} custom-call(s32[1]{0:T(128)} %bitcast.13.starts, f32[1]{0:T(128)S(6)} %tanh.3.gate, bf16[8192,1024]{1,0:T(8,128)(2,1)} %weight.7, bf16[128,1024]{1,0:T(8,128)(2,1)} %copy-done.8, bf16[128,1024]{1,0:T(8,128)(2,1)} %collective-permute-done.3.refs_1_, f32[256,1024]{1,0:T(8,128)S(1)} %project.5.refs_2_), custom_call_target="tpu_custom_call" | custom-call | tf_op jit(solution)/shard_map/project/pallas_call | solution.py:300
  112.5 0.7 copy-done.14
  113.1 0.1 copy-done.15
  113.3 3.2 %project.7 = bf16[256,1024]{1,0:T(8,128)(2,1)} custom-call(s32[1]{0:T(128)} %bitcast.starts, f32[1]{0:T(128)S(6)} %tanh.3.gate, bf16[8192,1024]{1,0:T(8,128)(2,1)} %weight.7, bf16[128,1024]{1,0:T(8,128)(2,1)} %copy-done.14, bf16[128,1024]{1,0:T(8,128)(2,1)} %copy-done.15, f32[256,1024]{1,0:T(8,128)S(1)} %project.6.refs_2_), custom_call_target="tpu_custom_call" | custom-call | tf_op jit(solution)/shard_map/project/pallas_call | solution.py:300
  (41 shorter events, 0.2 us)
Async XLA Ops:
  0.0 12.1 %copy-start = (bf16[1,6404,128]{2,1,0:T(8,128)(2,1)S(1)}, bf16[1,6404,128]{2,1,0:T(8,128)(2,1)}, u32[]{:S(2)}) copy-start(bf16[1,6404,128]{2,1,0:T(8,128)(2,1)} %img_keys.1) | copy-start | bytes 4918276
  3.5 26.0 %all-to-all-start = ((bf16[16,32,1152]{2,1,0:T(8,128)(2,1)}), bf16[16,32,1152]{2,1,0:T(8,128)(2,1)S(1)}, u32[]{:S(2)}, u32[]{:S(2)}) async-start(bf16[16,32,1152]{2,1,0:T(8,128)(2,1)} %bitcast.17), calls=%async_computation | async-start | bytes 2359296 | tf_op jit(solution)/shard_map/all_to_all | solution.py:326
  12.1 1.4 %copy-start.1 = (bf16[1,6404,128]{2,1,0:T(8,128)(2,1)S(1)}, bf16[1,6404,128]{2,1,0:T(8,128)(2,1)}, u32[]{:S(2)}) copy-start(bf16[1,6404,128]{2,1,0:T(8,128)(2,1)} %img_values.1) | copy-start | bytes 4918276
  15.5 1.7 %copy-start.2 = (bf16[4,1664,256]{2,1,0:T(8,128)(2,1)}, bf16[4,1664,256]{2,1,0:T(8,128)(2,1)S(1)}, u32[]{:S(2)}) copy-start(bf16[4,1664,256]{2,1,0:T(8,128)(2,1)S(1)} %get-tuple-element.23.keys_far) | copy-start | bytes 10223620
  17.2 1.3 %copy-start.3 = (bf16[4,144,1664]{2,1,0:T(8,128)(2,1)}, bf16[4,144,1664]{2,1,0:T(8,128)(2,1)S(1)}, u32[]{:S(2)}) copy-start(bf16[4,144,1664]{2,1,0:T(8,128)(2,1)S(1)} %get-tuple-element.24.values_far) | copy-start | bytes 5750788
  78.4 4.7 %collective-permute-start.6 = (bf16[128,1024]{1,0:T(8,128)(2,1)}, bf16[128,1024]{1,0:T(8,128)(2,1)S(1)}, u32[]{:S(2)}, u32[]{:S(2)}) collective-permute-start(bf16[128,1024]{1,0:T(8,128)(2,1)} %get-tuple-element.25.refs_0_), channel_id=1, source_target_pairs={{0,1},{1,0},{2,3},{3,2},{4,5},{5,4},{6,7},{7,6},{8,9},{9,8},{10,11... | collective-permute-start | bytes 786440 | tf_op jit(solution)/shard_map/ppermute | solution.py:333
  80.4 6.2 %collective-permute-start.7 = (bf16[128,1024]{1,0:T(8,128)(2,1)}, bf16[128,1024]{1,0:T(8,128)(2,1)S(1)}, u32[]{:S(2)}, u32[]{:S(2)}) collective-permute-start(bf16[128,1024]{1,0:T(8,128)(2,1)} %get-tuple-element.26.refs_1_), channel_id=1, source_target_pairs={{0,1},{1,0},{2,3},{3,2},{4,5},{5,4},{6,7},{7,6},{8,9},{9,8},{10,11... | collective-permute-start | bytes 786440 | tf_op jit(solution)/shard_map/ppermute | solution.py:333
  80.4 11.2 %collective-permute-start.5 = (bf16[128,1024]{1,0:T(8,128)(2,1)}, bf16[128,1024]{1,0:T(8,128)(2,1)S(1)}, u32[]{:S(2)}, u32[]{:S(2)}) collective-permute-start(bf16[128,1024]{1,0:T(8,128)(2,1)} %get-tuple-element.25.refs_0_), channel_id=1, source_target_pairs={{0,6},{1,7},{2,0},{3,1},{4,2},{5,3},{6,4},{7,5},{8,14},{9,15},{10,... | collective-permute-start | bytes 786440 | tf_op jit(solution)/shard_map/ppermute | solution.py:330
  82.9 8.7 %collective-permute-start = (bf16[128,1024]{1,0:T(8,128)(2,1)}, bf16[128,1024]{1,0:T(8,128)(2,1)S(1)}, u32[]{:S(2)}, u32[]{:S(2)}) collective-permute-start(bf16[128,1024]{1,0:T(8,128)(2,1)} %get-tuple-element.25.refs_0_), channel_id=1, source_target_pairs={{0,2},{1,3},{2,4},{3,5},{4,6},{5,7},{6,0},{7,1},{8,10},{9,11},{10,... | collective-permute-start | bytes 786440 | tf_op jit(solution)/shard_map/ppermute | solution.py:330
  82.9 14.1 %collective-permute-start.4 = (bf16[128,1024]{1,0:T(8,128)(2,1)}, bf16[128,1024]{1,0:T(8,128)(2,1)S(1)}, u32[]{:S(2)}, u32[]{:S(2)}) collective-permute-start(bf16[128,1024]{1,0:T(8,128)(2,1)} %get-tuple-element.26.refs_1_), channel_id=1, source_target_pairs={{0,2},{1,3},{2,4},{3,5},{4,6},{5,7},{6,0},{7,1},{8,10},{9,11},{10,... | collective-permute-start | bytes 786440 | tf_op jit(solution)/shard_map/ppermute | solution.py:330
  83.1 3.5 %copy-start.12 = (bf16[128,1024]{1,0:T(8,128)(2,1)}, bf16[128,1024]{1,0:T(8,128)(2,1)S(1)}, u32[]{:S(2)}) copy-start(bf16[128,1024]{1,0:T(8,128)(2,1)S(1)} %collective-permute-done.6.refs_2_) | copy-start | bytes 786436
  83.1 13.9 %collective-permute-start.2 = (bf16[128,1024]{1,0:T(8,128)(2,1)}, bf16[128,1024]{1,0:T(8,128)(2,1)S(1)}, u32[]{:S(2)}, u32[]{:S(2)}) collective-permute-start(bf16[128,1024]{1,0:T(8,128)(2,1)} %get-tuple-element.26.refs_1_), channel_id=1, source_target_pairs={{0,6},{1,7},{2,0},{3,1},{4,2},{5,3},{6,4},{7,5},{8,14},{9,15},{10,... | collective-permute-start | bytes 786440 | tf_op jit(solution)/shard_map/ppermute | solution.py:330
  86.6 0.7 copy-start.13
  91.6 11.9 %copy-start.5 = (bf16[128,1024]{1,0:T(8,128)(2,1)}, bf16[128,1024]{1,0:T(8,128)(2,1)S(1)}, u32[]{:S(2)}) copy-start(bf16[128,1024]{1,0:T(8,128)(2,1)S(1)} %collective-permute-done.5.refs_2_) | copy-start | bytes 786436
  91.6 11.9 %copy-start.4 = (bf16[128,1024]{1,0:T(8,128)(2,1)}, bf16[128,1024]{1,0:T(8,128)(2,1)S(1)}, u32[]{:S(2)}) copy-start(bf16[128,1024]{1,0:T(8,128)(2,1)S(1)} %collective-permute-done.refs_0_) | copy-start | bytes 786436
  96.9 6.6 %copy-start.7 = (bf16[128,1024]{1,0:T(8,128)(2,1)}, bf16[128,1024]{1,0:T(8,128)(2,1)S(1)}, u32[]{:S(2)}) copy-start(bf16[128,1024]{1,0:T(8,128)(2,1)S(1)} %collective-permute-done.4.refs_1_) | copy-start | bytes 786436
  96.9 6.6 %copy-start.6 = (bf16[128,1024]{1,0:T(8,128)(2,1)}, bf16[128,1024]{1,0:T(8,128)(2,1)S(1)}, u32[]{:S(2)}) copy-start(bf16[128,1024]{1,0:T(8,128)(2,1)S(1)} %collective-permute-done.2.refs_3_) | copy-start | bytes 786436
  96.9 2.9 %collective-permute-start.8 = (bf16[128,1024]{1,0:T(8,128)(2,1)S(1)}, bf16[128,1024]{1,0:T(8,128)(2,1)S(1)}, u32[]{:S(2)}, u32[]{:S(2)}) collective-permute-start(bf16[128,1024]{1,0:T(8,128)(2,1)S(1)} %collective-permute-done.refs_0_), channel_id=1, source_target_pairs={{0,1},{1,0},{2,3},{3,2},{4,5},{5,4},{6,7},{7,6},{8,9},{9,8},{10,11... | collective-permute-start | bytes 786440 | tf_op jit(solution)/shard_map/ppermute | solution.py:333
  98.7 3.4 %collective-permute-start.9 = (bf16[128,1024]{1,0:T(8,128)(2,1)S(1)}, bf16[128,1024]{1,0:T(8,128)(2,1)S(1)}, u32[]{:S(2)}, u32[]{:S(2)}) collective-permute-start(bf16[128,1024]{1,0:T(8,128)(2,1)S(1)} %collective-permute-done.4.refs_1_), channel_id=1, source_target_pairs={{0,1},{1,0},{2,3},{3,2},{4,5},{5,4},{6,7},{7,6},{8,9},{9,8},{10,11... | collective-permute-start | bytes 786440 | tf_op jit(solution)/shard_map/ppermute | solution.py:333
  98.8 3.3 %collective-permute-start.10 = (bf16[128,1024]{1,0:T(8,128)(2,1)S(1)}, bf16[128,1024]{1,0:T(8,128)(2,1)S(1)}, u32[]{:S(2)}, u32[]{:S(2)}) collective-permute-start(bf16[128,1024]{1,0:T(8,128)(2,1)S(1)} %collective-permute-done.5.refs_2_), channel_id=1, source_target_pairs={{0,1},{1,0},{2,3},{3,2},{4,5},{5,4},{6,7},{7,6},{8,9},{9,8},{10,11... | collective-permute-start | bytes 786440 | tf_op jit(solution)/shard_map/ppermute | solution.py:333
  99.2 4.3 %collective-permute-start.11 = (bf16[128,1024]{1,0:T(8,128)(2,1)S(1)}, bf16[128,1024]{1,0:T(8,128)(2,1)}, u32[]{:S(2)}, u32[]{:S(2)}) collective-permute-start(bf16[128,1024]{1,0:T(8,128)(2,1)S(1)} %collective-permute-done.2.refs_3_), channel_id=1, source_target_pairs={{0,1},{1,0},{2,3},{3,2},{4,5},{5,4},{6,7},{7,6},{8,9},{9,8},{10,11... | collective-permute-start | bytes 786440 | tf_op jit(solution)/shard_map/ppermute | solution.py:333
  99.3 9.5 %collective-permute-start.1 = (bf16[128,1024]{1,0:T(8,128)(2,1)S(1)}, bf16[128,1024]{1,0:T(8,128)(2,1)S(1)}, u32[]{:S(2)}, u32[]{:S(2)}) collective-permute-start(bf16[128,1024]{1,0:T(8,128)(2,1)S(1)} %collective-permute-done.refs_0_), channel_id=1, source_target_pairs={{0,2},{1,3},{2,4},{3,5},{4,6},{5,7},{6,0},{7,1},{8,10},{9,11},{10,... | collective-permute-start | bytes 786440 | tf_op jit(solution)/shard_map/ppermute | solution.py:330
  99.9 2.2 %copy-start.9 = (bf16[128,1024]{1,0:T(8,128)(2,1)}, bf16[128,1024]{1,0:T(8,128)(2,1)S(1)}, u32[]{:S(2)}) copy-start(bf16[128,1024]{1,0:T(8,128)(2,1)S(1)} %collective-permute-done.8.refs_4_) | copy-start | bytes 786436
  99.9 9.0 %collective-permute-start.3 = (bf16[128,1024]{1,0:T(8,128)(2,1)S(1)}, bf16[128,1024]{1,0:T(8,128)(2,1)}, u32[]{:S(2)}, u32[]{:S(2)}) collective-permute-start(bf16[128,1024]{1,0:T(8,128)(2,1)S(1)} %collective-permute-done.2.refs_3_), channel_id=1, source_target_pairs={{0,6},{1,7},{2,0},{3,1},{4,2},{5,3},{6,4},{7,5},{8,14},{9,15},{10,... | collective-permute-start | bytes 786440 | tf_op jit(solution)/shard_map/ppermute | solution.py:330
  102.1 0.7 copy-start.10
  102.8 0.7 copy-start.11
  108.9 1.2 %copy-start.8 = (bf16[128,1024]{1,0:T(8,128)(2,1)}, bf16[128,1024]{1,0:T(8,128)(2,1)S(1)}, u32[]{:S(2)}) copy-start(bf16[128,1024]{1,0:T(8,128)(2,1)S(1)} %collective-permute-done.1.refs_0_) | copy-start | bytes 786436
  108.9 3.6 %collective-permute-start.12 = (bf16[128,1024]{1,0:T(8,128)(2,1)S(1)}, bf16[128,1024]{1,0:T(8,128)(2,1)S(1)}, u32[]{:S(2)}, u32[]{:S(2)}) collective-permute-start(bf16[128,1024]{1,0:T(8,128)(2,1)S(1)} %collective-permute-done.1.refs_0_), channel_id=1, source_target_pairs={{0,1},{1,0},{2,3},{3,2},{4,5},{5,4},{6,7},{7,6},{8,9},{9,8},{10,11... | collective-permute-start | bytes 786440 | tf_op jit(solution)/shard_map/ppermute | solution.py:333
  109.9 2.5 %collective-permute-start.13 = (bf16[128,1024]{1,0:T(8,128)(2,1)}, bf16[128,1024]{1,0:T(8,128)(2,1)S(1)}, u32[]{:S(2)}, u32[]{:S(2)}) collective-permute-start(bf16[128,1024]{1,0:T(8,128)(2,1)} %collective-permute-done.3.refs_1_), channel_id=1, source_target_pairs={{0,1},{1,0},{2,3},{3,2},{4,5},{5,4},{6,7},{7,6},{8,9},{9,8},{10,11... | collective-permute-start | bytes 786440 | tf_op jit(solution)/shard_map/ppermute | solution.py:333
  112.4 0.7 copy-start.14
  112.5 0.8 copy-start.15

commit v3 on v2

--- a/solution.py
+++ b/solution.py
@@ -18,7 +18,8 @@
 BLOCK = 128
 CUTS = [(o, min(256, TP - o)) for o in range(0, TP, 256)]
 HUGE = 1e30
-UNROLL = 1
+UNROLL = 2
+HALVES = 2
 VM = pl.BlockSpec(memory_space=pltpu.VMEM)
 SM = pl.BlockSpec(memory_space=pltpu.SMEM)
 HB = pl.BlockSpec(memory_space=pltpu.HBM)
@@ -111,8 +112,13 @@
     )(near(place), img_keys, img_values)
 
 
-def attend_body(heads, recv, keys_far, values_far, out, *scratch):
-    keys, values, order, blocked, turned, seen, shift, acc, item_b, item_t, sems = scratch
+def attend_body(heads, half, *refs):
+    lead = half == 0
+    if lead:
+        recv, keys_far, values_far, out, order, tiles_out = refs[:6]
+    else:
+        recv, order, tiles_in, keys_far, values_far, out = refs[:6]
+    keys, values, blocked, turned, seen, shift, acc, item_b, item_t, sems = refs[6:]
     fetch_keys = pltpu.make_async_copy(keys_far, keys, sems.at[0])
     fetch_values = pltpu.make_async_copy(values_far, values, sems.at[1])
     fetch_keys.start()
@@ -121,17 +127,21 @@
     width = heads * HD
     blocks = slots // BLOCK
     lanes = heads * BLOCK
-    tile_i = jnp.concatenate([recv[:, width:].astype(f32)] * (slots // HD), axis=1)
-    tile_j = tile_i.T
-    i = lax.broadcasted_iota(i32, (slots, slots), 0)
-    j = lax.broadcasted_iota(i32, (slots, slots), 1)
-    before = (tile_j > tile_i) | ((tile_j == tile_i) & (j < i))
-    rank = jnp.sum(jnp.where(before, 1.0, 0.0), axis=1, keepdims=True)
-    placed = rank == j.astype(f32)
-    order[...] = jnp.where(placed, 1.0, 0.0).astype(bf16)
-    sorted_tiles = jnp.sum(jnp.where(placed, tile_i, 0.0), axis=0, keepdims=True)
+    if lead:
+        tile_i = jnp.concatenate([recv[:, HALVES * width :].astype(f32)] * (slots // HD), axis=1)
+        tile_j = tile_i.T
+        i = lax.broadcasted_iota(i32, (slots, slots), 0)
+        j = lax.broadcasted_iota(i32, (slots, slots), 1)
+        before = (tile_j > tile_i) | ((tile_j == tile_i) & (j < i))
+        rank = jnp.sum(jnp.where(before, 1.0, 0.0), axis=1, keepdims=True)
+        placed = rank == j.astype(f32)
+        order[...] = jnp.where(placed, 1.0, 0.0).astype(bf16)
+        sorted_tiles = jnp.sum(jnp.where(placed, tile_i, 0.0), axis=0, keepdims=True)
+        tiles_out[...] = jnp.broadcast_to(sorted_tiles, tiles_out.shape)
+    else:
+        sorted_tiles = tiles_in[:1, :]
     columns = lax.dot_general(
-        recv[:, :width], order[...], (((0,), (0,)), ((), ())), preferred_element_type=f32
+        recv[:, half * width : (half + 1) * width], order[...], (((0,), (0,)), ((), ())), preferred_element_type=f32
     ).astype(bf16)
     count = jnp.int32(0)
     for b in range(blocks):
@@ -209,21 +219,23 @@
     ).astype(bf16)
 
 
-def attend(recv, keys, values):
+def attend(half, recv, sorting, keys, values):
     slots = recv.shape[0]
-    width = recv.shape[1] - HD
+    width = (recv.shape[1] - HD) // HALVES
     heads = width // HD
     blocks = slots // BLOCK
     lanes = heads * BLOCK
-    return pl.pallas_call(
-        functools.partial(attend_body, heads),
-        out_shape=like((slots, width), bf16),
-        in_specs=[VM, HB, HB],
-        out_specs=VM,
+    outs = [like((slots, width), bf16)]
+    if half == 0:
+        outs += [like((slots, slots), bf16), like((8, slots), f32)]
+    return pl.pallas_call(
+        functools.partial(attend_body, heads, half),
+        out_shape=outs,
+        in_specs=[VM] * (1 + len(sorting)) + [HB, HB],
+        out_specs=[VM] * len(outs),
         scratch_shapes=[
             pltpu.VMEM(keys.shape, bf16),
             pltpu.VMEM(values.shape, bf16),
-            pltpu.VMEM((slots, slots), bf16),
             pltpu.VMEM((blocks, 2 * HD, lanes), bf16),
             pltpu.VMEM((width, slots), bf16),
             pltpu.VMEM((blocks, 8, lanes), f32),
@@ -240,74 +252,62 @@
             transcendentals=slots * heads * TP * TILES,
         ),
         name="attend",
-    )(recv, far(keys), far(values))
-
-
-def restore_body(back, returned, upper, lower):
-    rows = jnp.dot(back[...], returned[...], preferred_element_type=f32).astype(bf16)
-    half = upper.shape[0]
-    upper[...] = rows[:half]
-    lower[...] = rows[half:]
+    )(recv, *sorting, far(keys), far(values))
+
+
+def restore_body(back, returned, out):
+    out[...] = jnp.dot(back[...], returned[...], preferred_element_type=f32).astype(bf16)
 
 
 def restore(back, returned):
-    rows, width = back.shape[0], returned.shape[1]
     return pl.pallas_call(
         restore_body,
-        out_shape=[like((rows // 2, width), bf16)] * 2,
+        out_shape=pltpu.VMEM((back.shape[0], returned.shape[1]), bf16),
         in_specs=[VM, VM],
-        out_specs=[VM, VM],
+        out_specs=VM,
+        cost_estimate=pl.CostEstimate(flops=1, bytes_accessed=1, transcendentals=0),
         name="restore",
-    )(near(back), returned)
+    )(near(back), near(returned))
 
 
 def project_body(count, first, last, starts, gate, weight, *refs):
-    pieces = refs[: 2 * count]
-    before = None if first else refs[2 * count]
-    out, held, rows, sems = refs[-4:]
-    half, depth = pieces[0].shape
+    pieces = refs[:count]
+    before = None if first else refs[count]
+    out, held, sems = refs[-3:]
+    depth = pieces[0].shape[1]
 
     def fetch(n):
         start = pl.multiple_of(starts[n], depth)
-        return [
-            pltpu.make_async_copy(weight.at[pl.ds(start, depth), :], held.at[n], sems.at[3 * n]),
-            pltpu.make_async_copy(pieces[2 * n], rows.at[n, pl.ds(0, half), :], sems.at[3 * n + 1]),
-            pltpu.make_async_copy(pieces[2 * n + 1], rows.at[n, pl.ds(half, half), :], sems.at[3 * n + 2]),
-        ]
+        return pltpu.make_async_copy(weight.at[pl.ds(start, depth), :], held.at[n], sems.at[n])
 
     for n in range(count):
-        for copy in fetch(n):
-            copy.start()
+        fetch(n).start()
     total = None if first else before[...]
     for n in range(count):
-        for copy in fetch(n):
-            copy.wait()
-        term = jnp.dot(rows[n], held[n], preferred_element_type=f32)
+        fetch(n).wait()
+        term = jnp.dot(pieces[n][...], held[n], preferred_element_type=f32)
         total = term if total is None else total + term
     out[...] = (gate[0] * total).astype(bf16) if last else total
 
 
 def project(starts, gate, weight, pieces, before, last):
     count = len(pieces)
-    half, depth = pieces[0][0].shape
+    rows, depth = pieces[0].shape
     width = weight.shape[1]
-    given = [jnp.stack(starts).astype(i32), gate, far(weight)]
-    given += [far(x) for pair in pieces for x in pair]
-    spaces = [SM, SM] + [HB] * (1 + 2 * count)
+    given = [jnp.stack(starts).astype(i32), gate, far(weight), *[near(x) for x in pieces]]
     if before is not None:
         given.append(near(before))
-        spaces.append(VM)
     return pl.pallas_call(
         functools.partial(project_body, count, before is None, last),
-        out_shape=like((2 * half, width), bf16) if last else pltpu.VMEM((2 * half, width), f32),
-        in_specs=spaces,
+        out_shape=like((rows, width), bf16) if last else pltpu.VMEM((rows, width), f32),
+        in_specs=[SM, SM, HB] + [VM] * (len(given) - 3),
         out_specs=VM,
         scratch_shapes=[
             pltpu.VMEM((count, depth, width), bf16),
-            pltpu.VMEM((count, 2 * half, depth), bf16),
-            pltpu.SemaphoreType.DMA((3 * count,)),
+            pltpu.SemaphoreType.DMA((count,)),
         ],
-        compiler_params=pltpu.CompilerParams(vmem_limit_bytes=32 * 2**20),
+        compiler_params=pltpu.CompilerParams(vmem_limit_bytes=24 * 2**20),
+        cost_estimate=pl.CostEstimate(flops=1, bytes_accessed=1, transcendentals=0),
         name="project",
     )(*given)
 
@@ -332,37 +332,40 @@
     def other_core(x):
         return lax.ppermute(x, "tp", [(d, d ^ 1) for d in range(shares)])
 
-    def start(by, core):
+    part = width // HALVES
+
+    def start(by, core, half):
         share = (me - 2 * by) % shares
-        return (share ^ core) * width
-
-    def both(pair):
-        return [other_core(x) for x in pair]
-
+        return (share ^ core) * width + half * part
+
+    def spread(rows):
+        return [round_chips(rows, by) for by in hops]
+
+    def add(bys, cores, half, pieces, total, last=False):
+        starts = [start(by, core, half) for by, core in zip(bys, cores)]
+        return project(starts, gate, out_weight, pieces, total, last)
+
+    hops = (2, 1, chips - 1)
     send, place = dispatch(owners, lengths, row_counts, queries, slots)
     received = exchange(send)
     keys, values, back = cache(place, img_keys, img_values, slots)
-    upper, lower = restore(back, exchange(attend(received, keys, values)))
-    back_by = chips - 1
-    left_upper, right_lower = round_chips(upper, 1), round_chips(lower, back_by)
-    left_lower, right_upper = round_chips(lower, 1), round_chips(upper, back_by)
-    across = [round_chips(left_upper, 1), round_chips(right_lower, back_by)]
-    own = [upper, lower]
-    total = project([start(0, 0), start(0, 1)], gate, out_weight, [own, both(own)], None, False)
-    left, right = [left_upper, left_lower], [right_upper, right_lower]
-    left, right, total = lax.optimization_barrier((left, right, total))
-    total = project(
-        [start(1, 0), start(-1, 0), start(1, 1), start(-1, 1)],
-        gate,
-        out_weight,
-        [left, right, both(left), both(right)],
-        total,
-        False,
-    )
-    across, total = lax.optimization_barrier((across, total))
-    beside = both(across)
-    total = project([start(2, 0)], gate, out_weight, [across], total, False)
-    return project([start(2, 1)], gate, out_weight, [beside], total, True)
+    result, *sorting = attend(0, received, [], keys, values)
+    first = exchange(result)
+    (result,) = attend(1, received, sorting, keys, values)
+    first, result = lax.optimization_barrier((first, result))
+    second = exchange(result)
+    rows = restore(back, first)
+    pieces = [rows] + spread(rows)
+    rows = restore(back, second)
+    again = spread(rows)
+    pieces, _ = lax.optimization_barrier((pieces, rows))
+    total = add((0,) + hops, (0,) * 4, 0, pieces, None)
+    pieces = [other_core(x) for x in pieces]
+    total = add((0,) + hops, (1,) * 4, 0, pieces, total)
+    total = add((0, 0), (0, 1), 1, [rows, other_core(rows)], total)
+    again, total = lax.optimization_barrier((again, total))
+    again += [other_core(x) for x in again]
+    return add(hops + hops, (0,) * 3 + (1,) * 3, 1, again, total, True)
 
 
 def solution(mesh):

time: 115 us -> 112 us (0.974); the launches traced: 117 us -> 112 us
  blocking collectives: 31.5 us -> 0 us
  starting transfers between devices: 21.6 us -> 43.7 us
  waiting for transfers between devices: 16.9 us -> 22.5 us
  local copies, waits for them, and re-layouts: 7.33 us -> 4.51 us
  Pallas kernels: 37.3 us -> 39 us
    all_to_all x1 -> x0, blocking collectives: 31.5 us -> none  [exchange(): x = lax.all_to_all(x, 'grp', split_axis=0, concat_axis=0, tiled=True)]
    all_to_all x1 -> x3, starting transfers between devices: 8.6 us -> 30.3 us  [exchange(): x = lax.all_to_all(x, 'grp', split_axis=0, concat_axis=0, tiled=True)]
    all_to_all x1 -> x3, waiting for transfers between devices: 11 us -> 16.1 us  [exchange(): x = lax.all_to_all(x, 'grp', split_axis=0, concat_axis=0, tiled=True)]
    pallas_call x2 -> x4, Pallas kernels: 17.4 us -> 20.4 us  [the longest x2 19.8 us: attend(): pl.pallas_call(functools.partial(attend_body, heads, half), out_shape=out...]
    unnamed x32 -> x8, local copies, waits for them, and re-layouts: 7.33 us -> 4.43 us
    ppermute x6, starting transfers between devices: 7.53 us -> 9.97 us  [round_chips(): lax.ppermute(x, 'tp', [(d, (d + 2 * by) % shares) for d in range(shares)])]
    ppermute x8, starting transfers between devices: 5.48 us -> 3.5 us  [other_core(): return lax.ppermute(x, 'tp', [(d, d ^ 1) for d in range(shares)])]
    pallas_call x4, Pallas kernels: 15.2 us -> 13.9 us  [project(): pl.pallas_call(functools.partial(project_body, count, before is None, las...]
  transfers between devices with their start and end apart: 15 -> 17, of which waited for: 3 -> 7; matrix products, arithmetic and copies ran while one was open for 0% -> 0% of each run, Pallas kernels for 12% -> 19%
where the time goes in v3:
time: 112 us
  starting transfers between devices  43.7 us (39%)
  Pallas kernels  39 us (35%)
  waiting for transfers between devices  22.5 us (20%)
  local copies, waits for them, and re-layouts  4.51 us (4%)
  between operations  1.81 us (2%)
    all_to_all x3, starting transfers between devices, exchange(): x = lax.all_to_all(x, 'grp', split_axis=0, concat_axis=0, tiled=True)  30.3 us
    pallas_call x2, Pallas kernels, attend(): pl.pallas_call(functools.partial(attend_body, heads, half), out_shape=out...  19.8 us
    all_to_all x3, waiting for transfers between devices, exchange(): x = lax.all_to_all(x, 'grp', split_axis=0, concat_axis=0, tiled=True)  16.1 us
    pallas_call x4, Pallas kernels, project(): pl.pallas_call(functools.partial(project_body, count, before is None, las...  13.9 us
    ppermute x6, starting transfers between devices, round_chips(): lax.ppermute(x, 'tp', [(d, (d + 2 * by) % shares) for d in range(shares)])  9.97 us
    ppermute x6, waiting for transfers between devices, round_chips(): lax.ppermute(x, 'tp', [(d, (d + 2 * by) % shares) for d in range(shares)])  4.82 us
    unnamed x8, local copies, waits for them, and re-layouts  4.43 us
    ppermute x8, starting transfers between devices, other_core(): return lax.ppermute(x, 'tp', [(d, d ^ 1) for d in range(shares)])  3.5 us
  transfers between devices with their start and end apart: 17, of which 7 were waited for; matrix products, arithmetic and copies ran while one was open for 0% of the time, Pallas kernels for 19%

profile of v3, /device:TPU:1, one launch (start us, length us, event | category | flops | bytes accessed | tf_op | source)
XLA Modules:
  0.0 111.8 jit_solution(15145224170891508188)
XLA Ops:
  0.8 2.7 %dispatch.1 = (bf16[512,1152]{1,0:T(8,128)(2,1)}, f32[8,256]{1,0:T(8,128)S(1)}) custom-call(s32[1,256]{1,0:T(1,128)} %bitcast.29, s32[1,256]{1,0:T(1,128)} %bitcast.30, s32[1]{0:T(128)S(6)} %copy.9.counts, bf16[256,1024]{1,0:T(8,128)(2,1)} %queries.1), custom_call_target="tpu_custom_call" | custom-call | tf_op jit(solution)/shard_map/dispatch/pallas_call | solution.py:62
  3.5 8.6 %all-to-all-start = ((bf16[16,32,1152]{2,1,0:T(8,128)(2,1)}), bf16[16,32,1152]{2,1,0:T(8,128)(2,1)S(1)}, u32[]{:S(2)}, u32[]{:S(2)}) async-start(bf16[16,32,1152]{2,1,0:T(8,128)(2,1)} %bitcast.28), calls=%async_computation | async-start | bytes 2359296 | tf_op jit(solution)/shard_map/all_to_all | solution.py:326
  12.1 1.4 %copy-done.1 = bf16[1,6404,128]{2,1,0:T(8,128)(2,1)S(1)} copy-done((bf16[1,6404,128]{2,1,0:T(8,128)(2,1)S(1)}, bf16[1,6404,128]{2,1,0:T(8,128)(2,1)}, u32[]{:S(2)}) %copy-start.1) | copy-done | bytes 1639448
  13.6 2.0 %cache.1 = (bf16[4,1664,256]{2,1,0:T(8,128)(2,1)S(1)}, bf16[4,144,1664]{2,1,0:T(8,128)(2,1)S(1)}, bf16[256,512]{1,0:T(8,128)(2,1)S(1)}) custom-call(f32[8,256]{1,0:T(8,128)S(1)} %get-tuple-element.23.place, bf16[1,6404,128]{2,1,0:T(8,128)(2,1)S(1)} %copy-done, bf16[1,6404,128]{2,1,0:T(8,128)(2,1)S(1)} %copy-done.1), custom_call_target="tpu_custom_call" | custom-call | tf_op jit(solution)/shard_map/cache/pallas_call | solution.py:101
  15.6 1.7 %copy-done.2 = bf16[4,1664,256]{2,1,0:T(8,128)(2,1)} copy-done((bf16[4,1664,256]{2,1,0:T(8,128)(2,1)}, bf16[4,1664,256]{2,1,0:T(8,128)(2,1)S(1)}, u32[]{:S(2)}) %copy-start.2) | copy-done | bytes 3407896
  17.3 1.3 %copy-done.3 = bf16[4,144,1664]{2,1,0:T(8,128)(2,1)} copy-done((bf16[4,144,1664]{2,1,0:T(8,128)(2,1)}, bf16[4,144,1664]{2,1,0:T(8,128)(2,1)S(1)}, u32[]{:S(2)}) %copy-start.3) | copy-done | bytes 1916952
  18.6 11.0 %all-to-all-done = bf16[16,32,1152]{2,1,0:T(8,128)(2,1)S(1)} async-done(((bf16[16,32,1152]{2,1,0:T(8,128)(2,1)}), bf16[16,32,1152]{2,1,0:T(8,128)(2,1)S(1)}, u32[]{:S(2)}, u32[]{:S(2)}) %all-to-all-start) | async-done | bytes 1179680 | tf_op jit(solution)/shard_map/all_to_all | solution.py:326
  29.5 10.0 %attend.2 = (bf16[512,512]{1,0:T(8,128)(2,1)}, bf16[512,512]{1,0:T(8,128)(2,1)S(1)}, f32[8,512]{1,0:T(8,128)S(1)}) custom-call(bf16[512,1152]{1,0:T(8,128)(2,1)S(1)} %bitcast.26, bf16[4,1664,256]{2,1,0:T(8,128)(2,1)} %copy-done.2, bf16[4,144,1664]{2,1,0:T(8,128)(2,1)} %copy-done.3), custom_call_target="tpu_custom_call" | custom-call | flops 6979321856 | bytes 8388608 | tf_op jit(solution)/shard_map/attend/pallas_call | solution.py:231
  39.5 10.6 %all-to-all-start.1 = ((bf16[16,32,512]{2,1,0:T(8,128)(2,1)}), bf16[16,32,512]{2,1,0:T(8,128)(2,1)S(1)}, u32[]{:S(2)}, u32[]{:S(2)}) async-start(bf16[16,32,512]{2,1,0:T(8,128)(2,1)} %bitcast.10), calls=%async_computation.1 | async-start | bytes 1048576 | tf_op jit(solution)/shard_map/all_to_all | solution.py:326
  50.1 9.8 %attend.3 = bf16[512,512]{1,0:T(8,128)(2,1)} custom-call(bf16[512,1152]{1,0:T(8,128)(2,1)S(1)} %bitcast.27, bf16[512,512]{1,0:T(8,128)(2,1)S(1)} %get-tuple-element.29.refs_1_, f32[8,512]{1,0:T(8,128)S(1)} %get-tuple-element.30.refs_2_, bf16[4,1664,256]{2,1,0:T(8,128)(2,1)} %copy-done.2, bf16[4,144,1664]{2,1,0:T(8,128)(2,1)} %copy-done.3), custom_call_target="tpu_custom_call" | custom-call | flops 6979321856 | bytes 8388608 | tf_op jit(solution)/shard_map/attend/pallas_call | solution.py:231
  59.9 0.7 all-to-all-done.1
  60.6 11.1 %all-to-all-start.2 = ((bf16[16,32,512]{2,1,0:T(8,128)(2,1)}), bf16[16,32,512]{2,1,0:T(8,128)(2,1)S(1)}, u32[]{:S(2)}, u32[]{:S(2)}) async-start(bf16[16,32,512]{2,1,0:T(8,128)(2,1)} %bitcast.12), calls=%async_computation.2 | async-start | bytes 1048576 | tf_op jit(solution)/shard_map/all_to_all | solution.py:326
  71.7 0.3 restore.3.refs_0_
  72.0 2.8 %collective-permute-start.4 = (bf16[256,512]{1,0:T(8,128)(2,1)S(1)}, bf16[256,512]{1,0:T(8,128)(2,1)S(1)}, u32[]{:S(2)}, u32[]{:S(2)}) collective-permute-start(bf16[256,512]{1,0:T(8,128)(2,1)S(1)} %restore.3.refs_0_), channel_id=1, source_target_pairs={{0,4},{1,5},{2,6},{3,7},{4,0},{5,1},{6,2},{7,3},{8,12},{9,13},{10,... | collective-permute-start | bytes 786440 | tf_op jit(solution)/shard_map/ppermute | solution.py:330
  74.8 0.3 collective-permute-start.5
  75.2 2.4 %collective-permute-start.6 = (bf16[256,512]{1,0:T(8,128)(2,1)S(1)}, bf16[256,512]{1,0:T(8,128)(2,1)S(1)}, u32[]{:S(2)}, u32[]{:S(2)}) collective-permute-start(bf16[256,512]{1,0:T(8,128)(2,1)S(1)} %restore.3.refs_0_), channel_id=1, source_target_pairs={{0,6},{1,7},{2,0},{3,1},{4,2},{5,3},{6,4},{7,5},{8,14},{9,15},{10,... | collective-permute-start | bytes 786440 | tf_op jit(solution)/shard_map/ppermute | solution.py:330
  77.5 4.4 %all-to-all-done.2 = bf16[16,32,512]{2,1,0:T(8,128)(2,1)S(1)} async-done(((bf16[16,32,512]{2,1,0:T(8,128)(2,1)}), bf16[16,32,512]{2,1,0:T(8,128)(2,1)S(1)}, u32[]{:S(2)}, u32[]{:S(2)}) %all-to-all-start.2) | async-done | bytes 524320 | tf_op jit(solution)/shard_map/all_to_all | solution.py:326
  82.3 4.8 %collective-permute-done.5.refs_2_ = bf16[256,512]{1,0:T(8,128)(2,1)S(1)} collective-permute-done((bf16[256,512]{1,0:T(8,128)(2,1)S(1)}, bf16[256,512]{1,0:T(8,128)(2,1)S(1)}, u32[]{:S(2)}, u32[]{:S(2)}) %collective-permute-start.5) | collective-permute-done | bytes 262176 | tf_op jit(solution)/shard_map/ppermute | solution.py:330
  87.1 1.0 collective-permute-start.10
  88.0 0.5 collective-permute-start.8
  88.5 1.8 %collective-permute-start = (bf16[256,512]{1,0:T(8,128)(2,1)S(1)}, bf16[256,512]{1,0:T(8,128)(2,1)S(1)}, u32[]{:S(2)}, u32[]{:S(2)}) collective-permute-start(bf16[256,512]{1,0:T(8,128)(2,1)S(1)} %restore.2.refs_0_), channel_id=1, source_target_pairs={{0,4},{1,5},{2,6},{3,7},{4,0},{5,1},{6,2},{7,3},{8,12},{9,13},{10,... | collective-permute-start | bytes 786440 | tf_op jit(solution)/shard_map/ppermute | solution.py:330
  90.3 1.2 %collective-permute-start.1 = (bf16[256,512]{1,0:T(8,128)(2,1)S(1)}, bf16[256,512]{1,0:T(8,128)(2,1)S(1)}, u32[]{:S(2)}, u32[]{:S(2)}) collective-permute-start(bf16[256,512]{1,0:T(8,128)(2,1)S(1)} %restore.2.refs_0_), channel_id=1, source_target_pairs={{0,2},{1,3},{2,4},{3,5},{4,6},{5,7},{6,0},{7,1},{8,10},{9,11},{10,... | collective-permute-start | bytes 786440 | tf_op jit(solution)/shard_map/ppermute | solution.py:330
  91.5 1.5 %collective-permute-start.2 = (bf16[256,512]{1,0:T(8,128)(2,1)S(1)}, bf16[256,512]{1,0:T(8,128)(2,1)S(1)}, u32[]{:S(2)}, u32[]{:S(2)}) collective-permute-start(bf16[256,512]{1,0:T(8,128)(2,1)S(1)} %restore.2.refs_0_), channel_id=1, source_target_pairs={{0,6},{1,7},{2,0},{3,1},{4,2},{5,3},{6,4},{7,5},{8,14},{9,15},{10,... | collective-permute-start | bytes 786440 | tf_op jit(solution)/shard_map/ppermute | solution.py:330
  93.0 1.3 %collective-permute-start.9 = (bf16[256,512]{1,0:T(8,128)(2,1)S(1)}, bf16[256,512]{1,0:T(8,128)(2,1)S(1)}, u32[]{:S(2)}, u32[]{:S(2)}) collective-permute-start(bf16[256,512]{1,0:T(8,128)(2,1)S(1)} %collective-permute-done.5.refs_2_), channel_id=1, source_target_pairs={{0,1},{1,0},{2,3},{3,2},{4,5},{5,4},{6,7},{7,6},{8,9},{9,8},{10,11... | collective-permute-start | bytes 786440 | tf_op jit(solution)/shard_map/ppermute | solution.py:333
  95.3 3.5 %project.4.refs_4_ = f32[256,1024]{1,0:T(8,128)S(1)} custom-call(s32[4]{0:T(128)S(1)} %pad_add_fusion.2.starts, f32[1]{0:T(128)S(6)} %tanh.3.gate, bf16[8192,1024]{1,0:T(8,128)(2,1)} %weight.7, bf16[256,512]{1,0:T(8,128)(2,1)S(1)} %restore.3.refs_0_, bf16[256,512]{1,0:T(8,128)(2,1)S(1)} %collective-permute-done.4.refs_1_, ...), custom_call_target="tpu_custom_call" | custom-call | flops 1 | bytes 1 | tf_op jit(solution)/shard_map/project/pallas_call | solution.py:300
  98.8 3.2 %project.5.refs_2_ = f32[256,1024]{1,0:T(8,128)S(1)} custom-call(s32[4]{0:T(128)S(1)} %pad_add_fusion.1.starts, f32[1]{0:T(128)S(6)} %tanh.3.gate, bf16[8192,1024]{1,0:T(8,128)(2,1)} %weight.7, bf16[256,512]{1,0:T(8,128)(2,1)S(1)} %collective-permute-done.7.refs_0_, bf16[256,512]{1,0:T(8,128)(2,1)S(1)} %collective-permute-done.8.refs_1_, ...), custom_call_target="tpu_custom_call" | custom-call | flops 1 | bytes 1 | tf_op jit(solution)/shard_map/project/pallas_call | solution.py:300
  102.0 2.6 %project.6.refs_6_ = f32[256,1024]{1,0:T(8,128)S(1)} custom-call(s32[2]{0:T(128)S(1)} %pad_add_fusion.starts, f32[1]{0:T(128)S(6)} %tanh.3.gate, bf16[8192,1024]{1,0:T(8,128)(2,1)} %weight.7, bf16[256,512]{1,0:T(8,128)(2,1)S(1)} %restore.2.refs_0_, bf16[256,512]{1,0:T(8,128)(2,1)S(1)} %collective-permute-done.3.refs_1_, f32[256,1024]{1,0:T(8,128)S(1)} %project.5.refs_2_), custom_call_target="tpu_custom_call" | custom-call | flops 1 | bytes 1 | tf_op jit(solution)/shard_map/project/pallas_call | solution.py:300
  104.7 0.5 collective-permute-start.12
  105.4 0.8 collective-permute-done.11.refs_3_
  106.2 0.4 collective-permute-done.12.refs_4_
  106.6 0.4 collective-permute-done.13.refs_5_
  107.0 4.7 %project.7 = bf16[256,1024]{1,0:T(8,128)(2,1)} custom-call(s32[6]{0:T(128)S(1)} %stack.66.starts, f32[1]{0:T(128)S(6)} %tanh.3.gate, bf16[8192,1024]{1,0:T(8,128)(2,1)} %weight.7, bf16[256,512]{1,0:T(8,128)(2,1)S(1)} %collective-permute-done.refs_0_, bf16[256,512]{1,0:T(8,128)(2,1)S(1)} %collective-permute-done.1.refs_1_, ...), custom_call_target="tpu_custom_call" | custom-call | flops 1 | bytes 1 | tf_op jit(solution)/shard_map/project/pallas_call | solution.py:300
  (24 shorter events, 0.8 us)
Async XLA Ops:
  0.0 12.1 %copy-start = (bf16[1,6404,128]{2,1,0:T(8,128)(2,1)S(1)}, bf16[1,6404,128]{2,1,0:T(8,128)(2,1)}, u32[]{:S(2)}) copy-start(bf16[1,6404,128]{2,1,0:T(8,128)(2,1)} %img_keys.1) | copy-start | bytes 4918276
  3.5 26.0 %all-to-all-start = ((bf16[16,32,1152]{2,1,0:T(8,128)(2,1)}), bf16[16,32,1152]{2,1,0:T(8,128)(2,1)S(1)}, u32[]{:S(2)}, u32[]{:S(2)}) async-start(bf16[16,32,1152]{2,1,0:T(8,128)(2,1)} %bitcast.28), calls=%async_computation | async-start | bytes 2359296 | tf_op jit(solution)/shard_map/all_to_all | solution.py:326
  12.1 1.4 %copy-start.1 = (bf16[1,6404,128]{2,1,0:T(8,128)(2,1)S(1)}, bf16[1,6404,128]{2,1,0:T(8,128)(2,1)}, u32[]{:S(2)}) copy-start(bf16[1,6404,128]{2,1,0:T(8,128)(2,1)} %img_values.1) | copy-start | bytes 4918276
  15.5 1.7 %copy-start.2 = (bf16[4,1664,256]{2,1,0:T(8,128)(2,1)}, bf16[4,1664,256]{2,1,0:T(8,128)(2,1)S(1)}, u32[]{:S(2)}) copy-start(bf16[4,1664,256]{2,1,0:T(8,128)(2,1)S(1)} %get-tuple-element.26.refs_1_.refs_3_) | copy-start | bytes 10223620
  17.3 1.3 %copy-start.3 = (bf16[4,144,1664]{2,1,0:T(8,128)(2,1)}, bf16[4,144,1664]{2,1,0:T(8,128)(2,1)S(1)}, u32[]{:S(2)}) copy-start(bf16[4,144,1664]{2,1,0:T(8,128)(2,1)S(1)} %get-tuple-element.27.refs_2_.refs_4_) | copy-start | bytes 5750788
  39.5 21.1 %all-to-all-start.1 = ((bf16[16,32,512]{2,1,0:T(8,128)(2,1)}), bf16[16,32,512]{2,1,0:T(8,128)(2,1)S(1)}, u32[]{:S(2)}, u32[]{:S(2)}) async-start(bf16[16,32,512]{2,1,0:T(8,128)(2,1)} %bitcast.10), calls=%async_computation.1 | async-start | bytes 1048576 | tf_op jit(solution)/shard_map/all_to_all | solution.py:326
  60.6 21.3 %all-to-all-start.2 = ((bf16[16,32,512]{2,1,0:T(8,128)(2,1)}), bf16[16,32,512]{2,1,0:T(8,128)(2,1)S(1)}, u32[]{:S(2)}, u32[]{:S(2)}) async-start(bf16[16,32,512]{2,1,0:T(8,128)(2,1)} %bitcast.12), calls=%async_computation.2 | async-start | bytes 1048576 | tf_op jit(solution)/shard_map/all_to_all | solution.py:326
  72.0 10.2 %collective-permute-start.4 = (bf16[256,512]{1,0:T(8,128)(2,1)S(1)}, bf16[256,512]{1,0:T(8,128)(2,1)S(1)}, u32[]{:S(2)}, u32[]{:S(2)}) collective-permute-start(bf16[256,512]{1,0:T(8,128)(2,1)S(1)} %restore.3.refs_0_), channel_id=1, source_target_pairs={{0,4},{1,5},{2,6},{3,7},{4,0},{5,1},{6,2},{7,3},{8,12},{9,13},{10,... | collective-permute-start | bytes 786440 | tf_op jit(solution)/shard_map/ppermute | solution.py:330
  74.8 12.2 %collective-permute-start.5 = (bf16[256,512]{1,0:T(8,128)(2,1)S(1)}, bf16[256,512]{1,0:T(8,128)(2,1)S(1)}, u32[]{:S(2)}, u32[]{:S(2)}) collective-permute-start(bf16[256,512]{1,0:T(8,128)(2,1)S(1)} %restore.3.refs_0_), channel_id=1, source_target_pairs={{0,2},{1,3},{2,4},{3,5},{4,6},{5,7},{6,0},{7,1},{8,10},{9,11},{10,... | collective-permute-start | bytes 786440 | tf_op jit(solution)/shard_map/ppermute | solution.py:330
  75.2 11.9 %collective-permute-start.6 = (bf16[256,512]{1,0:T(8,128)(2,1)S(1)}, bf16[256,512]{1,0:T(8,128)(2,1)S(1)}, u32[]{:S(2)}, u32[]{:S(2)}) collective-permute-start(bf16[256,512]{1,0:T(8,128)(2,1)S(1)} %restore.3.refs_0_), channel_id=1, source_target_pairs={{0,6},{1,7},{2,0},{3,1},{4,2},{5,3},{6,4},{7,5},{8,14},{9,15},{10,... | collective-permute-start | bytes 786440 | tf_op jit(solution)/shard_map/ppermute | solution.py:330
  87.1 3.3 %collective-permute-start.10 = (bf16[256,512]{1,0:T(8,128)(2,1)S(1)}, bf16[256,512]{1,0:T(8,128)(2,1)S(1)}, u32[]{:S(2)}, u32[]{:S(2)}) collective-permute-start(bf16[256,512]{1,0:T(8,128)(2,1)S(1)} %collective-permute-done.6.refs_3_), channel_id=1, source_target_pairs={{0,1},{1,0},{2,3},{3,2},{4,5},{5,4},{6,7},{7,6},{8,9},{9,8},{10,11... | collective-permute-start | bytes 786440 | tf_op jit(solution)/shard_map/ppermute | solution.py:333
  88.0 3.5 %collective-permute-start.7 = (bf16[256,512]{1,0:T(8,128)(2,1)S(1)}, bf16[256,512]{1,0:T(8,128)(2,1)S(1)}, u32[]{:S(2)}, u32[]{:S(2)}) collective-permute-start(bf16[256,512]{1,0:T(8,128)(2,1)S(1)} %restore.3.refs_0_), channel_id=1, source_target_pairs={{0,1},{1,0},{2,3},{3,2},{4,5},{5,4},{6,7},{7,6},{8,9},{9,8},{10,11... | collective-permute-start | bytes 786440 | tf_op jit(solution)/shard_map/ppermute | solution.py:333
  88.0 5.0 %collective-permute-start.8 = (bf16[256,512]{1,0:T(8,128)(2,1)S(1)}, bf16[256,512]{1,0:T(8,128)(2,1)S(1)}, u32[]{:S(2)}, u32[]{:S(2)}) collective-permute-start(bf16[256,512]{1,0:T(8,128)(2,1)S(1)} %collective-permute-done.4.refs_1_), channel_id=1, source_target_pairs={{0,1},{1,0},{2,3},{3,2},{4,5},{5,4},{6,7},{7,6},{8,9},{9,8},{10,11... | collective-permute-start | bytes 786440 | tf_op jit(solution)/shard_map/ppermute | solution.py:333
  88.5 13.5 %collective-permute-start.3 = (bf16[256,512]{1,0:T(8,128)(2,1)S(1)}, bf16[256,512]{1,0:T(8,128)(2,1)S(1)}, u32[]{:S(2)}, u32[]{:S(2)}) collective-permute-start(bf16[256,512]{1,0:T(8,128)(2,1)S(1)} %restore.2.refs_0_), channel_id=1, source_target_pairs={{0,1},{1,0},{2,3},{3,2},{4,5},{5,4},{6,7},{7,6},{8,9},{9,8},{10,11... | collective-permute-start | bytes 786440 | tf_op jit(solution)/shard_map/ppermute | solution.py:333
  88.5 16.1 %collective-permute-start = (bf16[256,512]{1,0:T(8,128)(2,1)S(1)}, bf16[256,512]{1,0:T(8,128)(2,1)S(1)}, u32[]{:S(2)}, u32[]{:S(2)}) collective-permute-start(bf16[256,512]{1,0:T(8,128)(2,1)S(1)} %restore.2.refs_0_), channel_id=1, source_target_pairs={{0,4},{1,5},{2,6},{3,7},{4,0},{5,1},{6,2},{7,3},{8,12},{9,13},{10,... | collective-permute-start | bytes 786440 | tf_op jit(solution)/shard_map/ppermute | solution.py:330
  90.3 14.3 %collective-permute-start.1 = (bf16[256,512]{1,0:T(8,128)(2,1)S(1)}, bf16[256,512]{1,0:T(8,128)(2,1)S(1)}, u32[]{:S(2)}, u32[]{:S(2)}) collective-permute-start(bf16[256,512]{1,0:T(8,128)(2,1)S(1)} %restore.2.refs_0_), channel_id=1, source_target_pairs={{0,2},{1,3},{2,4},{3,5},{4,6},{5,7},{6,0},{7,1},{8,10},{9,11},{10,... | collective-permute-start | bytes 786440 | tf_op jit(solution)/shard_map/ppermute | solution.py:330
  91.5 13.1 %collective-permute-start.2 = (bf16[256,512]{1,0:T(8,128)(2,1)S(1)}, bf16[256,512]{1,0:T(8,128)(2,1)S(1)}, u32[]{:S(2)}, u32[]{:S(2)}) collective-permute-start(bf16[256,512]{1,0:T(8,128)(2,1)S(1)} %restore.2.refs_0_), channel_id=1, source_target_pairs={{0,6},{1,7},{2,0},{3,1},{4,2},{5,3},{6,4},{7,5},{8,14},{9,15},{10,... | collective-permute-start | bytes 786440 | tf_op jit(solution)/shard_map/ppermute | solution.py:330
  93.0 5.8 %collective-permute-start.9 = (bf16[256,512]{1,0:T(8,128)(2,1)S(1)}, bf16[256,512]{1,0:T(8,128)(2,1)S(1)}, u32[]{:S(2)}, u32[]{:S(2)}) collective-permute-start(bf16[256,512]{1,0:T(8,128)(2,1)S(1)} %collective-permute-done.5.refs_2_), channel_id=1, source_target_pairs={{0,1},{1,0},{2,3},{3,2},{4,5},{5,4},{6,7},{7,6},{8,9},{9,8},{10,11... | collective-permute-start | bytes 786440 | tf_op jit(solution)/shard_map/ppermute | solution.py:333
  104.6 1.6 %collective-permute-start.11 = (bf16[256,512]{1,0:T(8,128)(2,1)S(1)}, bf16[256,512]{1,0:T(8,128)(2,1)S(1)}, u32[]{:S(2)}, u32[]{:S(2)}) collective-permute-start(bf16[256,512]{1,0:T(8,128)(2,1)S(1)} %collective-permute-done.refs_0_), channel_id=1, source_target_pairs={{0,1},{1,0},{2,3},{3,2},{4,5},{5,4},{6,7},{7,6},{8,9},{9,8},{10,11... | collective-permute-start | bytes 786440 | tf_op jit(solution)/shard_map/ppermute | solution.py:333
  104.7 1.9 %collective-permute-start.12 = (bf16[256,512]{1,0:T(8,128)(2,1)S(1)}, bf16[256,512]{1,0:T(8,128)(2,1)S(1)}, u32[]{:S(2)}, u32[]{:S(2)}) collective-permute-start(bf16[256,512]{1,0:T(8,128)(2,1)S(1)} %collective-permute-done.1.refs_1_), channel_id=1, source_target_pairs={{0,1},{1,0},{2,3},{3,2},{4,5},{5,4},{6,7},{7,6},{8,9},{9,8},{10,11... | collective-permute-start | bytes 786440 | tf_op jit(solution)/shard_map/ppermute | solution.py:333
  105.2 1.8 %collective-permute-start.13 = (bf16[256,512]{1,0:T(8,128)(2,1)S(1)}, bf16[256,512]{1,0:T(8,128)(2,1)S(1)}, u32[]{:S(2)}, u32[]{:S(2)}) collective-permute-start(bf16[256,512]{1,0:T(8,128)(2,1)S(1)} %collective-permute-done.2.refs_2_), channel_id=1, source_target_pairs={{0,1},{1,0},{2,3},{3,2},{4,5},{5,4},{6,7},{7,6},{8,9},{9,8},{10,11... | collective-permute-start | bytes 786440 | tf_op jit(solution)/shard_map/ppermute | solution.py:333

commit v4 on v3

--- a/solution.py
+++ b/solution.py
@@ -18,7 +18,6 @@
 BLOCK = 128
 CUTS = [(o, min(256, TP - o)) for o in range(0, TP, 256)]
 HUGE = 1e30
-UNROLL = 2
 HALVES = 2
 VM = pl.BlockSpec(memory_space=pltpu.VMEM)
 SM = pl.BlockSpec(memory_space=pltpu.SMEM)
@@ -156,9 +155,6 @@
             item_b[count] = b
             item_t[count] = t
             count = count + jnp.where(t < most, 1, 0)
-    for u in range(UNROLL):
-        item_b[count + u] = 0
-        item_t[count + u] = TILES
     acc[...] = jnp.zeros_like(acc)
 
     def score(t, o, w, query):
@@ -174,16 +170,20 @@
     fetch_values.wait()
 
     def work(b, t):
-        tile = jnp.minimum(t, TILES - 1)
         query = blocked[b]
         moved = jnp.where(seen[b, :1, :] > t.astype(f32), shift[b, :1, :], HUGE)
-        weights = [jnp.exp2(score(tile, o, w, query) - moved).astype(bf16) for o, w in CUTS]
-        acc[b] += jnp.dot(values[tile], jnp.concatenate(weights, axis=0), preferred_element_type=f32)
-
-    @pl.loop(0, (count + UNROLL - 1) // UNROLL)
+        weights = [jnp.exp2(score(t, o, w, query) - moved).astype(bf16) for o, w in CUTS]
+        acc[b] += jnp.dot(values[t], jnp.concatenate(weights, axis=0), preferred_element_type=f32)
+
+    @pl.loop(0, count // 2)
     def _(n):
-        for u in range(UNROLL):
-            work(item_b[UNROLL * n + u], item_t[UNROLL * n + u])
+        for u in range(2):
+            work(item_b[2 * n + u], item_t[2 * n + u])
+
+    @pl.when(count % 2 == 1)
+    def _():
+        work(item_b[count - 1], item_t[count - 1])
+
 
     unsafe = jnp.max(jnp.where(acc[:, HD : HD + 1, :] < HUGE, 0.0, 1.0))
 
@@ -241,8 +241,8 @@
             pltpu.VMEM((blocks, 8, lanes), f32),
             pltpu.VMEM((blocks, 8, lanes), f32),
             pltpu.VMEM((blocks, VR, lanes), f32),
-            pltpu.SMEM((blocks * TILES + UNROLL,), i32),
-            pltpu.SMEM((blocks * TILES + UNROLL,), i32),
+            pltpu.SMEM((blocks * TILES + 1,), i32),
+            pltpu.SMEM((blocks * TILES + 1,), i32),
             pltpu.SemaphoreType.DMA((2,)),
         ],
         compiler_params=pltpu.CompilerParams(vmem_limit_bytes=42 * 2**20),

time: 112 us -> 107 us (0.955)
  waiting for transfers between devices: 22.5 us -> 18 us
    all_to_all x3, starting transfers between devices: 30.3 us -> 26.4 us  [exchange(): x = lax.all_to_all(x, 'grp', split_axis=0, concat_axis=0, tiled=True)]
    ppermute x8, starting transfers between devices: 3.5 us -> 7.28 us  [other_core(): return lax.ppermute(x, 'tp', [(d, d ^ 1) for d in range(shares)])]
    ppermute x6, waiting for transfers between devices: 4.82 us -> 1.94 us  [round_chips(): lax.ppermute(x, 'tp', [(d, (d + 2 * by) % shares) for d in range(shares)])]
    all_to_all x3, waiting for transfers between devices: 16.1 us -> 14.5 us  [exchange(): x = lax.all_to_all(x, 'grp', split_axis=0, concat_axis=0, tiled=True)]
  transfers between devices with their start and end apart: 17 -> 17, of which waited for: 7 -> 7; matrix products, arithmetic and copies ran while one was open for 0% -> 0% of each run, Pallas kernels for 19% -> 20%
where the time goes in v4:
time: 107 us
  starting transfers between devices  43.7 us (41%)
  Pallas kernels  39.1 us (37%)
  waiting for transfers between devices  18 us (17%)
  local copies, waits for them, and re-layouts  4.51 us (4%)
  between operations  1.82 us (2%)
    all_to_all x3, starting transfers between devices, exchange(): x = lax.all_to_all(x, 'grp', split_axis=0, concat_axis=0, tiled=True)  26.4 us
    pallas_call x2, Pallas kernels, attend(): pl.pallas_call(functools.partial(attend_body, heads, half), out_shape=out...  19.9 us
    all_to_all x3, waiting for transfers between devices, exchange(): x = lax.all_to_all(x, 'grp', split_axis=0, concat_axis=0, tiled=True)  14.5 us
    pallas_call x4, Pallas kernels, project(): pl.pallas_call(functools.partial(project_body, count, before is None, las...  13.9 us
    ppermute x6, starting transfers between devices, round_chips(): lax.ppermute(x, 'tp', [(d, (d + 2 * by) % shares) for d in range(shares)])  9.99 us
    ppermute x8, starting transfers between devices, other_core(): return lax.ppermute(x, 'tp', [(d, d ^ 1) for d in range(shares)])  7.28 us
    unnamed x8, local copies, waits for them, and re-layouts  4.43 us
    pallas_call x1, Pallas kernels, dispatch(): pl.pallas_call(dispatch_body, out_shape=[like((slots, width + HD), bf16),...  2.73 us
  transfers between devices with their start and end apart: 17, of which 7 were waited for; matrix products, arithmetic and copies ran while one was open for 0% of the time, Pallas kernels for 20%

profile of v4, /device:TPU:1, one launch (start us, length us, event | category | flops | bytes accessed | tf_op | source)
XLA Modules:
  0.0 107.4 jit_solution(7979166515251340473)
XLA Ops:
  0.8 2.7 %dispatch.1 = (bf16[512,1152]{1,0:T(8,128)(2,1)}, f32[8,256]{1,0:T(8,128)S(1)}) custom-call(s32[1,256]{1,0:T(1,128)} %bitcast.29, s32[1,256]{1,0:T(1,128)} %bitcast.30, s32[1]{0:T(128)S(6)} %copy.9.counts, bf16[256,1024]{1,0:T(8,128)(2,1)} %queries.1), custom_call_target="tpu_custom_call" | custom-call | tf_op jit(solution)/shard_map/dispatch/pallas_call | solution.py:61
  3.5 8.6 %all-to-all-start = ((bf16[16,32,1152]{2,1,0:T(8,128)(2,1)}), bf16[16,32,1152]{2,1,0:T(8,128)(2,1)S(1)}, u32[]{:S(2)}, u32[]{:S(2)}) async-start(bf16[16,32,1152]{2,1,0:T(8,128)(2,1)} %bitcast.28), calls=%async_computation | async-start | bytes 2359296 | tf_op jit(solution)/shard_map/all_to_all | solution.py:326
  12.1 1.4 %copy-done.1 = bf16[1,6404,128]{2,1,0:T(8,128)(2,1)S(1)} copy-done((bf16[1,6404,128]{2,1,0:T(8,128)(2,1)S(1)}, bf16[1,6404,128]{2,1,0:T(8,128)(2,1)}, u32[]{:S(2)}) %copy-start.1) | copy-done | bytes 1639448
  13.6 2.0 %cache.1 = (bf16[4,1664,256]{2,1,0:T(8,128)(2,1)S(1)}, bf16[4,144,1664]{2,1,0:T(8,128)(2,1)S(1)}, bf16[256,512]{1,0:T(8,128)(2,1)S(1)}) custom-call(f32[8,256]{1,0:T(8,128)S(1)} %get-tuple-element.23.place, bf16[1,6404,128]{2,1,0:T(8,128)(2,1)S(1)} %copy-done, bf16[1,6404,128]{2,1,0:T(8,128)(2,1)S(1)} %copy-done.1), custom_call_target="tpu_custom_call" | custom-call | tf_op jit(solution)/shard_map/cache/pallas_call | solution.py:100
  15.6 1.7 %copy-done.2 = bf16[4,1664,256]{2,1,0:T(8,128)(2,1)} copy-done((bf16[4,1664,256]{2,1,0:T(8,128)(2,1)}, bf16[4,1664,256]{2,1,0:T(8,128)(2,1)S(1)}, u32[]{:S(2)}) %copy-start.2) | copy-done | bytes 3407896
  17.3 1.3 %copy-done.3 = bf16[4,144,1664]{2,1,0:T(8,128)(2,1)} copy-done((bf16[4,144,1664]{2,1,0:T(8,128)(2,1)}, bf16[4,144,1664]{2,1,0:T(8,128)(2,1)S(1)}, u32[]{:S(2)}) %copy-start.3) | copy-done | bytes 1916952
  18.6 11.0 %all-to-all-done = bf16[16,32,1152]{2,1,0:T(8,128)(2,1)S(1)} async-done(((bf16[16,32,1152]{2,1,0:T(8,128)(2,1)}), bf16[16,32,1152]{2,1,0:T(8,128)(2,1)S(1)}, u32[]{:S(2)}, u32[]{:S(2)}) %all-to-all-start) | async-done | bytes 1179680 | tf_op jit(solution)/shard_map/all_to_all | solution.py:326
  29.5 10.0 %attend.2 = (bf16[512,512]{1,0:T(8,128)(2,1)}, bf16[512,512]{1,0:T(8,128)(2,1)S(1)}, f32[8,512]{1,0:T(8,128)S(1)}) custom-call(bf16[512,1152]{1,0:T(8,128)(2,1)S(1)} %bitcast.26, bf16[4,1664,256]{2,1,0:T(8,128)(2,1)} %copy-done.2, bf16[4,144,1664]{2,1,0:T(8,128)(2,1)} %copy-done.3), custom_call_target="tpu_custom_call" | custom-call | flops 6979321856 | bytes 8388608 | tf_op jit(solution)/shard_map/attend/pallas_call | solution.py:231
  39.5 7.2 %all-to-all-start.1 = ((bf16[16,32,512]{2,1,0:T(8,128)(2,1)}), bf16[16,32,512]{2,1,0:T(8,128)(2,1)S(1)}, u32[]{:S(2)}, u32[]{:S(2)}) async-start(bf16[16,32,512]{2,1,0:T(8,128)(2,1)} %bitcast.10), calls=%async_computation.1 | async-start | bytes 1048576 | tf_op jit(solution)/shard_map/all_to_all | solution.py:326
  46.7 9.9 %attend.3 = bf16[512,512]{1,0:T(8,128)(2,1)} custom-call(bf16[512,1152]{1,0:T(8,128)(2,1)S(1)} %bitcast.27, bf16[512,512]{1,0:T(8,128)(2,1)S(1)} %get-tuple-element.29.refs_1_, f32[8,512]{1,0:T(8,128)S(1)} %get-tuple-element.30.refs_2_, bf16[4,1664,256]{2,1,0:T(8,128)(2,1)} %copy-done.2, bf16[4,144,1664]{2,1,0:T(8,128)(2,1)} %copy-done.3), custom_call_target="tpu_custom_call" | custom-call | flops 6979321856 | bytes 8388608 | tf_op jit(solution)/shard_map/attend/pallas_call | solution.py:231
  56.6 10.7 %all-to-all-start.2 = ((bf16[16,32,512]{2,1,0:T(8,128)(2,1)}), bf16[16,32,512]{2,1,0:T(8,128)(2,1)S(1)}, u32[]{:S(2)}, u32[]{:S(2)}) async-start(bf16[16,32,512]{2,1,0:T(8,128)(2,1)} %bitcast.12), calls=%async_computation.2 | async-start | bytes 1048576 | tf_op jit(solution)/shard_map/all_to_all | solution.py:326
  67.3 0.3 restore.3.refs_0_
  67.6 2.8 %collective-permute-start.4 = (bf16[256,512]{1,0:T(8,128)(2,1)S(1)}, bf16[256,512]{1,0:T(8,128)(2,1)S(1)}, u32[]{:S(2)}, u32[]{:S(2)}) collective-permute-start(bf16[256,512]{1,0:T(8,128)(2,1)S(1)} %restore.3.refs_0_), channel_id=1, source_target_pairs={{0,4},{1,5},{2,6},{3,7},{4,0},{5,1},{6,2},{7,3},{8,12},{9,13},{10,... | collective-permute-start | bytes 786440 | tf_op jit(solution)/shard_map/ppermute | solution.py:330
  70.4 0.3 collective-permute-start.5
  70.7 2.4 %collective-permute-start.6 = (bf16[256,512]{1,0:T(8,128)(2,1)S(1)}, bf16[256,512]{1,0:T(8,128)(2,1)S(1)}, u32[]{:S(2)}, u32[]{:S(2)}) collective-permute-start(bf16[256,512]{1,0:T(8,128)(2,1)S(1)} %restore.3.refs_0_), channel_id=1, source_target_pairs={{0,6},{1,7},{2,0},{3,1},{4,2},{5,3},{6,4},{7,5},{8,14},{9,15},{10,... | collective-permute-start | bytes 786440 | tf_op jit(solution)/shard_map/ppermute | solution.py:330
  73.1 3.5 %all-to-all-done.2 = bf16[16,32,512]{2,1,0:T(8,128)(2,1)S(1)} async-done(((bf16[16,32,512]{2,1,0:T(8,128)(2,1)}), bf16[16,32,512]{2,1,0:T(8,128)(2,1)S(1)}, u32[]{:S(2)}, u32[]{:S(2)}) %all-to-all-start.2) | async-done | bytes 524320 | tf_op jit(solution)/shard_map/all_to_all | solution.py:326
  76.6 0.3 restore.2.refs_0_
  76.9 1.9 %collective-permute-done.5.refs_2_ = bf16[256,512]{1,0:T(8,128)(2,1)S(1)} collective-permute-done((bf16[256,512]{1,0:T(8,128)(2,1)S(1)}, bf16[256,512]{1,0:T(8,128)(2,1)S(1)}, u32[]{:S(2)}, u32[]{:S(2)}) %collective-permute-start.5) | collective-permute-done | bytes 262176 | tf_op jit(solution)/shard_map/ppermute | solution.py:330
  78.9 4.7 %collective-permute-start.10 = (bf16[256,512]{1,0:T(8,128)(2,1)S(1)}, bf16[256,512]{1,0:T(8,128)(2,1)S(1)}, u32[]{:S(2)}, u32[]{:S(2)}) collective-permute-start(bf16[256,512]{1,0:T(8,128)(2,1)S(1)} %collective-permute-done.6.refs_3_), channel_id=1, source_target_pairs={{0,1},{1,0},{2,3},{3,2},{4,5},{5,4},{6,7},{7,6},{8,9},{9,8},{10,11... | collective-permute-start | bytes 786440 | tf_op jit(solution)/shard_map/ppermute | solution.py:333
  83.6 0.5 collective-permute-start.8
  84.1 1.8 %collective-permute-start = (bf16[256,512]{1,0:T(8,128)(2,1)S(1)}, bf16[256,512]{1,0:T(8,128)(2,1)S(1)}, u32[]{:S(2)}, u32[]{:S(2)}) collective-permute-start(bf16[256,512]{1,0:T(8,128)(2,1)S(1)} %restore.2.refs_0_), channel_id=1, source_target_pairs={{0,4},{1,5},{2,6},{3,7},{4,0},{5,1},{6,2},{7,3},{8,12},{9,13},{10,... | collective-permute-start | bytes 786440 | tf_op jit(solution)/shard_map/ppermute | solution.py:330
  85.9 1.1 %collective-permute-start.1 = (bf16[256,512]{1,0:T(8,128)(2,1)S(1)}, bf16[256,512]{1,0:T(8,128)(2,1)S(1)}, u32[]{:S(2)}, u32[]{:S(2)}) collective-permute-start(bf16[256,512]{1,0:T(8,128)(2,1)S(1)} %restore.2.refs_0_), channel_id=1, source_target_pairs={{0,2},{1,3},{2,4},{3,5},{4,6},{5,7},{6,0},{7,1},{8,10},{9,11},{10,... | collective-permute-start | bytes 786440 | tf_op jit(solution)/shard_map/ppermute | solution.py:330
  87.1 1.5 %collective-permute-start.2 = (bf16[256,512]{1,0:T(8,128)(2,1)S(1)}, bf16[256,512]{1,0:T(8,128)(2,1)S(1)}, u32[]{:S(2)}, u32[]{:S(2)}) collective-permute-start(bf16[256,512]{1,0:T(8,128)(2,1)S(1)} %restore.2.refs_0_), channel_id=1, source_target_pairs={{0,6},{1,7},{2,0},{3,1},{4,2},{5,3},{6,4},{7,5},{8,14},{9,15},{10,... | collective-permute-start | bytes 786440 | tf_op jit(solution)/shard_map/ppermute | solution.py:330
  88.6 1.3 %collective-permute-start.9 = (bf16[256,512]{1,0:T(8,128)(2,1)S(1)}, bf16[256,512]{1,0:T(8,128)(2,1)S(1)}, u32[]{:S(2)}, u32[]{:S(2)}) collective-permute-start(bf16[256,512]{1,0:T(8,128)(2,1)S(1)} %collective-permute-done.5.refs_2_), channel_id=1, source_target_pairs={{0,1},{1,0},{2,3},{3,2},{4,5},{5,4},{6,7},{7,6},{8,9},{9,8},{10,11... | collective-permute-start | bytes 786440 | tf_op jit(solution)/shard_map/ppermute | solution.py:333
  90.9 3.5 %project.4.refs_4_ = f32[256,1024]{1,0:T(8,128)S(1)} custom-call(s32[4]{0:T(128)S(1)} %pad_add_fusion.2.starts, f32[1]{0:T(128)S(6)} %tanh.3.gate, bf16[8192,1024]{1,0:T(8,128)(2,1)} %weight.7, bf16[256,512]{1,0:T(8,128)(2,1)S(1)} %restore.3.refs_0_, bf16[256,512]{1,0:T(8,128)(2,1)S(1)} %collective-permute-done.4.refs_1_, ...), custom_call_target="tpu_custom_call" | custom-call | flops 1 | bytes 1 | tf_op jit(solution)/shard_map/project/pallas_call | solution.py:300
  94.4 3.2 %project.5.refs_2_ = f32[256,1024]{1,0:T(8,128)S(1)} custom-call(s32[4]{0:T(128)S(1)} %pad_add_fusion.1.starts, f32[1]{0:T(128)S(6)} %tanh.3.gate, bf16[8192,1024]{1,0:T(8,128)(2,1)} %weight.7, bf16[256,512]{1,0:T(8,128)(2,1)S(1)} %collective-permute-done.7.refs_0_, bf16[256,512]{1,0:T(8,128)(2,1)S(1)} %collective-permute-done.8.refs_1_, ...), custom_call_target="tpu_custom_call" | custom-call | flops 1 | bytes 1 | tf_op jit(solution)/shard_map/project/pallas_call | solution.py:300
  97.6 2.6 %project.6.refs_6_ = f32[256,1024]{1,0:T(8,128)S(1)} custom-call(s32[2]{0:T(128)S(1)} %pad_add_fusion.starts, f32[1]{0:T(128)S(6)} %tanh.3.gate, bf16[8192,1024]{1,0:T(8,128)(2,1)} %weight.7, bf16[256,512]{1,0:T(8,128)(2,1)S(1)} %restore.2.refs_0_, bf16[256,512]{1,0:T(8,128)(2,1)S(1)} %collective-permute-done.3.refs_1_, f32[256,1024]{1,0:T(8,128)S(1)} %project.5.refs_2_), custom_call_target="tpu_custom_call" | custom-call | flops 1 | bytes 1 | tf_op jit(solution)/shard_map/project/pallas_call | solution.py:300
  100.3 0.5 collective-permute-start.12
  101.0 0.8 collective-permute-done.11.refs_3_
  101.8 0.4 collective-permute-done.12.refs_4_
  102.2 0.4 collective-permute-done.13.refs_5_
  102.6 4.7 %project.7 = bf16[256,1024]{1,0:T(8,128)(2,1)} custom-call(s32[6]{0:T(128)S(1)} %stack.66.starts, f32[1]{0:T(128)S(6)} %tanh.3.gate, bf16[8192,1024]{1,0:T(8,128)(2,1)} %weight.7, bf16[256,512]{1,0:T(8,128)(2,1)S(1)} %collective-permute-done.refs_0_, bf16[256,512]{1,0:T(8,128)(2,1)S(1)} %collective-permute-done.1.refs_1_, ...), custom_call_target="tpu_custom_call" | custom-call | flops 1 | bytes 1 | tf_op jit(solution)/shard_map/project/pallas_call | solution.py:300
  (24 shorter events, 0.6 us)
Async XLA Ops:
  0.0 12.1 %copy-start = (bf16[1,6404,128]{2,1,0:T(8,128)(2,1)S(1)}, bf16[1,6404,128]{2,1,0:T(8,128)(2,1)}, u32[]{:S(2)}) copy-start(bf16[1,6404,128]{2,1,0:T(8,128)(2,1)} %img_keys.1) | copy-start | bytes 4918276
  3.5 26.0 %all-to-all-start = ((bf16[16,32,1152]{2,1,0:T(8,128)(2,1)}), bf16[16,32,1152]{2,1,0:T(8,128)(2,1)S(1)}, u32[]{:S(2)}, u32[]{:S(2)}) async-start(bf16[16,32,1152]{2,1,0:T(8,128)(2,1)} %bitcast.28), calls=%async_computation | async-start | bytes 2359296 | tf_op jit(solution)/shard_map/all_to_all | solution.py:326
  12.1 1.4 %copy-start.1 = (bf16[1,6404,128]{2,1,0:T(8,128)(2,1)S(1)}, bf16[1,6404,128]{2,1,0:T(8,128)(2,1)}, u32[]{:S(2)}) copy-start(bf16[1,6404,128]{2,1,0:T(8,128)(2,1)} %img_values.1) | copy-start | bytes 4918276
  15.5 1.7 %copy-start.2 = (bf16[4,1664,256]{2,1,0:T(8,128)(2,1)}, bf16[4,1664,256]{2,1,0:T(8,128)(2,1)S(1)}, u32[]{:S(2)}) copy-start(bf16[4,1664,256]{2,1,0:T(8,128)(2,1)S(1)} %get-tuple-element.26.refs_1_.refs_3_) | copy-start | bytes 10223620
  17.3 1.3 %copy-start.3 = (bf16[4,144,1664]{2,1,0:T(8,128)(2,1)}, bf16[4,144,1664]{2,1,0:T(8,128)(2,1)S(1)}, u32[]{:S(2)}) copy-start(bf16[4,144,1664]{2,1,0:T(8,128)(2,1)S(1)} %get-tuple-element.27.refs_2_.refs_4_) | copy-start | bytes 5750788
  39.5 17.1 %all-to-all-start.1 = ((bf16[16,32,512]{2,1,0:T(8,128)(2,1)}), bf16[16,32,512]{2,1,0:T(8,128)(2,1)S(1)}, u32[]{:S(2)}, u32[]{:S(2)}) async-start(bf16[16,32,512]{2,1,0:T(8,128)(2,1)} %bitcast.10), calls=%async_computation.1 | async-start | bytes 1048576 | tf_op jit(solution)/shard_map/all_to_all | solution.py:326
  56.6 20.0 %all-to-all-start.2 = ((bf16[16,32,512]{2,1,0:T(8,128)(2,1)}), bf16[16,32,512]{2,1,0:T(8,128)(2,1)S(1)}, u32[]{:S(2)}, u32[]{:S(2)}) async-start(bf16[16,32,512]{2,1,0:T(8,128)(2,1)} %bitcast.12), calls=%async_computation.2 | async-start | bytes 1048576 | tf_op jit(solution)/shard_map/all_to_all | solution.py:326
  67.6 9.3 %collective-permute-start.4 = (bf16[256,512]{1,0:T(8,128)(2,1)S(1)}, bf16[256,512]{1,0:T(8,128)(2,1)S(1)}, u32[]{:S(2)}, u32[]{:S(2)}) collective-permute-start(bf16[256,512]{1,0:T(8,128)(2,1)S(1)} %restore.3.refs_0_), channel_id=1, source_target_pairs={{0,4},{1,5},{2,6},{3,7},{4,0},{5,1},{6,2},{7,3},{8,12},{9,13},{10,... | collective-permute-start | bytes 786440 | tf_op jit(solution)/shard_map/ppermute | solution.py:330
  70.4 8.4 %collective-permute-start.5 = (bf16[256,512]{1,0:T(8,128)(2,1)S(1)}, bf16[256,512]{1,0:T(8,128)(2,1)S(1)}, u32[]{:S(2)}, u32[]{:S(2)}) collective-permute-start(bf16[256,512]{1,0:T(8,128)(2,1)S(1)} %restore.3.refs_0_), channel_id=1, source_target_pairs={{0,2},{1,3},{2,4},{3,5},{4,6},{5,7},{6,0},{7,1},{8,10},{9,11},{10,... | collective-permute-start | bytes 786440 | tf_op jit(solution)/shard_map/ppermute | solution.py:330
  70.7 8.1 %collective-permute-start.6 = (bf16[256,512]{1,0:T(8,128)(2,1)S(1)}, bf16[256,512]{1,0:T(8,128)(2,1)S(1)}, u32[]{:S(2)}, u32[]{:S(2)}) collective-permute-start(bf16[256,512]{1,0:T(8,128)(2,1)S(1)} %restore.3.refs_0_), channel_id=1, source_target_pairs={{0,6},{1,7},{2,0},{3,1},{4,2},{5,3},{6,4},{7,5},{8,14},{9,15},{10,... | collective-permute-start | bytes 786440 | tf_op jit(solution)/shard_map/ppermute | solution.py:330
  78.9 7.1 %collective-permute-start.10 = (bf16[256,512]{1,0:T(8,128)(2,1)S(1)}, bf16[256,512]{1,0:T(8,128)(2,1)S(1)}, u32[]{:S(2)}, u32[]{:S(2)}) collective-permute-start(bf16[256,512]{1,0:T(8,128)(2,1)S(1)} %collective-permute-done.6.refs_3_), channel_id=1, source_target_pairs={{0,1},{1,0},{2,3},{3,2},{4,5},{5,4},{6,7},{7,6},{8,9},{9,8},{10,11... | collective-permute-start | bytes 786440 | tf_op jit(solution)/shard_map/ppermute | solution.py:333
  83.6 3.5 %collective-permute-start.7 = (bf16[256,512]{1,0:T(8,128)(2,1)S(1)}, bf16[256,512]{1,0:T(8,128)(2,1)S(1)}, u32[]{:S(2)}, u32[]{:S(2)}) collective-permute-start(bf16[256,512]{1,0:T(8,128)(2,1)S(1)} %restore.3.refs_0_), channel_id=1, source_target_pairs={{0,1},{1,0},{2,3},{3,2},{4,5},{5,4},{6,7},{7,6},{8,9},{9,8},{10,11... | collective-permute-start | bytes 786440 | tf_op jit(solution)/shard_map/ppermute | solution.py:333
  83.6 5.0 %collective-permute-start.8 = (bf16[256,512]{1,0:T(8,128)(2,1)S(1)}, bf16[256,512]{1,0:T(8,128)(2,1)S(1)}, u32[]{:S(2)}, u32[]{:S(2)}) collective-permute-start(bf16[256,512]{1,0:T(8,128)(2,1)S(1)} %collective-permute-done.4.refs_1_), channel_id=1, source_target_pairs={{0,1},{1,0},{2,3},{3,2},{4,5},{5,4},{6,7},{7,6},{8,9},{9,8},{10,11... | collective-permute-start | bytes 786440 | tf_op jit(solution)/shard_map/ppermute | solution.py:333
  84.1 13.5 %collective-permute-start.3 = (bf16[256,512]{1,0:T(8,128)(2,1)S(1)}, bf16[256,512]{1,0:T(8,128)(2,1)S(1)}, u32[]{:S(2)}, u32[]{:S(2)}) collective-permute-start(bf16[256,512]{1,0:T(8,128)(2,1)S(1)} %restore.2.refs_0_), channel_id=1, source_target_pairs={{0,1},{1,0},{2,3},{3,2},{4,5},{5,4},{6,7},{7,6},{8,9},{9,8},{10,11... | collective-permute-start | bytes 786440 | tf_op jit(solution)/shard_map/ppermute | solution.py:333
  84.1 16.1 %collective-permute-start = (bf16[256,512]{1,0:T(8,128)(2,1)S(1)}, bf16[256,512]{1,0:T(8,128)(2,1)S(1)}, u32[]{:S(2)}, u32[]{:S(2)}) collective-permute-start(bf16[256,512]{1,0:T(8,128)(2,1)S(1)} %restore.2.refs_0_), channel_id=1, source_target_pairs={{0,4},{1,5},{2,6},{3,7},{4,0},{5,1},{6,2},{7,3},{8,12},{9,13},{10,... | collective-permute-start | bytes 786440 | tf_op jit(solution)/shard_map/ppermute | solution.py:330
  85.9 14.3 %collective-permute-start.1 = (bf16[256,512]{1,0:T(8,128)(2,1)S(1)}, bf16[256,512]{1,0:T(8,128)(2,1)S(1)}, u32[]{:S(2)}, u32[]{:S(2)}) collective-permute-start(bf16[256,512]{1,0:T(8,128)(2,1)S(1)} %restore.2.refs_0_), channel_id=1, source_target_pairs={{0,2},{1,3},{2,4},{3,5},{4,6},{5,7},{6,0},{7,1},{8,10},{9,11},{10,... | collective-permute-start | bytes 786440 | tf_op jit(solution)/shard_map/ppermute | solution.py:330
  87.1 13.1 %collective-permute-start.2 = (bf16[256,512]{1,0:T(8,128)(2,1)S(1)}, bf16[256,512]{1,0:T(8,128)(2,1)S(1)}, u32[]{:S(2)}, u32[]{:S(2)}) collective-permute-start(bf16[256,512]{1,0:T(8,128)(2,1)S(1)} %restore.2.refs_0_), channel_id=1, source_target_pairs={{0,6},{1,7},{2,0},{3,1},{4,2},{5,3},{6,4},{7,5},{8,14},{9,15},{10,... | collective-permute-start | bytes 786440 | tf_op jit(solution)/shard_map/ppermute | solution.py:330
  88.6 5.8 %collective-permute-start.9 = (bf16[256,512]{1,0:T(8,128)(2,1)S(1)}, bf16[256,512]{1,0:T(8,128)(2,1)S(1)}, u32[]{:S(2)}, u32[]{:S(2)}) collective-permute-start(bf16[256,512]{1,0:T(8,128)(2,1)S(1)} %collective-permute-done.5.refs_2_), channel_id=1, source_target_pairs={{0,1},{1,0},{2,3},{3,2},{4,5},{5,4},{6,7},{7,6},{8,9},{9,8},{10,11... | collective-permute-start | bytes 786440 | tf_op jit(solution)/shard_map/ppermute | solution.py:333
  100.2 1.6 %collective-permute-start.11 = (bf16[256,512]{1,0:T(8,128)(2,1)S(1)}, bf16[256,512]{1,0:T(8,128)(2,1)S(1)}, u32[]{:S(2)}, u32[]{:S(2)}) collective-permute-start(bf16[256,512]{1,0:T(8,128)(2,1)S(1)} %collective-permute-done.refs_0_), channel_id=1, source_target_pairs={{0,1},{1,0},{2,3},{3,2},{4,5},{5,4},{6,7},{7,6},{8,9},{9,8},{10,11... | collective-permute-start | bytes 786440 | tf_op jit(solution)/shard_map/ppermute | solution.py:333
  100.3 1.9 %collective-permute-start.12 = (bf16[256,512]{1,0:T(8,128)(2,1)S(1)}, bf16[256,512]{1,0:T(8,128)(2,1)S(1)}, u32[]{:S(2)}, u32[]{:S(2)}) collective-permute-start(bf16[256,512]{1,0:T(8,128)(2,1)S(1)} %collective-permute-done.1.refs_1_), channel_id=1, source_target_pairs={{0,1},{1,0},{2,3},{3,2},{4,5},{5,4},{6,7},{7,6},{8,9},{9,8},{10,11... | collective-permute-start | bytes 786440 | tf_op jit(solution)/shard_map/ppermute | solution.py:333
  100.8 1.8 %collective-permute-start.13 = (bf16[256,512]{1,0:T(8,128)(2,1)S(1)}, bf16[256,512]{1,0:T(8,128)(2,1)S(1)}, u32[]{:S(2)}, u32[]{:S(2)}) collective-permute-start(bf16[256,512]{1,0:T(8,128)(2,1)S(1)} %collective-permute-done.2.refs_2_), channel_id=1, source_target_pairs={{0,1},{1,0},{2,3},{3,2},{4,5},{5,4},{6,7},{7,6},{8,9},{9,8},{10,11... | collective-permute-start | bytes 786440 | tf_op jit(solution)/shard_map/ppermute | solution.py:333
